TPU v7x, 512 devices: a whole 4x4x16 slice. The times are simulated.
512 devices in a mesh: grp: 32 (over z, core), vocab: 16 (over x, y).
Axes of the slice: x: 4, y: 4, z: 16, core: 2. Of those that a mesh axis runs over, the one named last changes fastest.
Arguments:
- student_hidden: bfloat16 [512, 5120], P('grp', 'vocab'), may hold values from -120 to 120
- teacher_hidden: bfloat16 [768, 5120], P('grp', 'vocab'), may hold values from -120 to 120
- student_head: bfloat16 [77824, 5120], P(('grp', 'vocab')), may hold values from -0.5 to 0.5
- teacher_head: bfloat16 [77824, 5120], P(('grp', 'vocab')), may hold values from -0.5 to 0.5
- route: int32 [32, 3], replicated, may hold values from 0 to 64, as said below
Outputs:
- head_grad: bfloat16 [77824, 5120], P(('grp', 'vocab'))
- token_kl: float32 [512], P('grp')
Inputs may be any that keep to these rules, and one draw needn't show every extreme that they name: route[g, b] is the student block held by slot block b of teacher group g, or 64 for an empty slot; every student block is held exactly once; student block 2 s is held by teacher group s and block 2 s + 1 by teacher group s - 1 or s + 1 (cyclically); a teacher group holds 1 to 3 blocks.
All inputs are finite; a program needn't handle non-finite values.
Results may differ from a plain program's by a relative error of at most 0.015.
Values may be sent and summed in bfloat16 or wider, within the bound.
No kernel may reach another device: no remote copies, remote signals or barrier semaphores. Data moves between devices by JAX's collectives and lax.ppermute only.
A program may use at most 64 MiB of HBM per device.

v0:
```python
import jax
import jax.numpy as jnp
from jax import lax
from jax.sharding import PartitionSpec as P

TASKS = 8


def block_sources(route, groups, tasks, block_rows, total_tokens):
    flat_route = route.reshape(-1)
    block_count = 2 * groups
    block_ids = jnp.arange(block_count, dtype=jnp.int32)
    slot_ids = jnp.arange(flat_route.shape[0], dtype=jnp.int32)
    hits = flat_route[None, :] == block_ids[:, None]
    source = jnp.sum(jnp.where(hits, slot_ids[None, :], 0), axis=1)
    per_task = groups // tasks
    slot_task = slot_ids // route.shape[1] // per_task
    task_ids = jnp.arange(tasks, dtype=jnp.int32)
    alive = flat_route < block_count
    task_blocks = jnp.sum(
        jnp.where((slot_task[None, :] == task_ids[:, None]) & alive[None, :], 1, 0), axis=1
    ).astype(jnp.int32)
    source_task = source // route.shape[1] // per_task
    owning = jnp.sum(
        jnp.where(source_task[:, None] == task_ids[None, :], task_blocks[None, :], 0), axis=1
    )
    block_weight = total_tokens / (tasks * block_rows * owning.astype(jnp.float32))
    weight = jnp.repeat(block_weight, block_rows)
    return (source, weight)


def per_device(student_hidden, teacher_hidden, student_head, teacher_head, route):
    groups = lax.axis_size("grp")
    group_index = lax.axis_index("grp")
    rows_group = student_hidden.shape[0]
    block_rows = rows_group // 2
    total_tokens = rows_group * groups
    slot_count = route.shape[0] * route.shape[1]
    vocab_rows = student_head.shape[0]
    source, weight = block_sources(route, groups, TASKS, block_rows, total_tokens)
    student_cols = lax.all_gather(student_hidden, "vocab", axis=1, tiled=True)
    student_all = lax.all_gather(student_cols, "grp", axis=0, tiled=True)
    student_logits = jnp.einsum(
        "vd,td->vt", student_head, student_all, preferred_element_type=jnp.float32
    )
    slot_cols = lax.all_gather(teacher_hidden, "vocab", axis=1, tiled=True)
    slot_logits = jnp.einsum(
        "vd,td->vt",
        teacher_head,
        lax.all_gather(slot_cols, "grp", axis=0, tiled=True),
        preferred_element_type=jnp.float32,
    )
    teacher_logits = jnp.take(
        slot_logits.reshape(vocab_rows, slot_count, block_rows), source, axis=1
    ).reshape(vocab_rows, total_tokens)
    teacher_local = jnp.max(teacher_logits, axis=0)
    student_local = jnp.max(student_logits, axis=0)
    teacher_top, student_top = lax.pmax((teacher_local, student_local), ("grp", "vocab"))
    teacher_exp = jnp.exp(teacher_logits - teacher_top[None, :])
    student_exp = jnp.exp(student_logits - student_top[None, :])
    teacher_total, student_total, cross_total = lax.psum(
        (
            jnp.sum(teacher_exp, axis=0),
            jnp.sum(student_exp, axis=0),
            jnp.sum(teacher_exp * (teacher_logits - student_logits), axis=0),
        ),
        ("grp", "vocab"),
    )
    teacher_prob = teacher_exp / teacher_total[None, :]
    student_prob = student_exp / student_total[None, :]
    teacher_lse = teacher_top + jnp.log(teacher_total)
    student_lse = student_top + jnp.log(student_total)
    token_loss = cross_total / teacher_total - teacher_lse + student_lse
    logit_grad = (weight[None, :] * (student_prob - teacher_prob)).astype(jnp.bfloat16)
    head_grad = jnp.dot(logit_grad, student_all, preferred_element_type=jnp.float32).astype(
        jnp.bfloat16
    )
    own_loss = lax.dynamic_slice_in_dim(token_loss, group_index * rows_group, rows_group, 0)
    return (head_grad, own_loss)


def solution(mesh):
    return jax.shard_map(
        per_device,
        mesh=mesh,
        in_specs=(
            P("grp", "vocab"),
            P("grp", "vocab"),
            P(("grp", "vocab"), None),
            P(("grp", "vocab"), None),
            P(),
        ),
        out_specs=(P(("grp", "vocab"), None), P("grp")),
        check_vma=False,
    )
```

profile of v0, /device:TPU:1, one launch (start us, length us, event | category | flops | bytes accessed | tf_op | source)
XLA Modules:
  0.0 411.0 jit_solution(4025759586177159528)
XLA Ops:
  7.2 19.8 %all-gather = bf16[16,320,16]{1,2,0:T(8,128)(2,1)S(1)} all-gather(bf16[1,320,16]{1,2,0:T(8,128)(2,1)} %bitcast.35), channel_id=1, replica_groups=mesh['grp'=32,'vocab'=16] {'vocab'}, dimensions={0}, use_global_device_ids=true | all-gather | bytes 174080 | tf_op jit(solution)/shard_map/all_gather | solution.py:41
  27.1 0.8 reshape.120
  28.0 17.8 %all-gather.1 = bf16[16,320,24]{1,2,0:T(8,128)(2,1)S(1)} all-gather(bf16[1,320,24]{1,2,0:T(8,128)(2,1)} %bitcast.34), channel_id=1, replica_groups=mesh['grp'=32,'vocab'=16] {'vocab'}, dimensions={0}, use_global_device_ids=true | all-gather | bytes 261120 | tf_op jit(solution)/shard_map/all_gather | solution.py:46
  45.9 0.9 reshape.122
  46.8 0.8 copy.18
  47.6 0.1 eq.20
  47.7 0.1 select_reduce_fusion
  47.9 0.1 broadcast_in_dim.73
  48.0 0.1 select_reduce_fusion.2
  48.4 0.1 mul.24
  48.5 63.4 %all-gather.5.cloned.1.call-done = bf16[512,5120]{1,0:T(8,128)(2,1)} async-done(((bf16[16,5120]{1,0:T(8,128)(2,1)}), bf16[512,5120]{1,0:T(8,128)(2,1)}) %all-gather.5.cloned.1.call-update) | async-done | bytes 5242896 | tf_op jit(solution)/shard_map/all_gather | solution.py:42
  111.9 4.9 %fusion.12 = (f32[512]{0:T(512)S(1)}, f32[152,512]{1,0:T(8,128)S(1)}) fusion(bf16[152,5120]{1,0:T(8,128)(2,1)} %param.7, bf16[512,5120]{1,0:T(8,128)(2,1)} %all-gather.5.cloned.1.call-done), kind=kOutput, calls=%fused_computation.47 | convolution fusion | flops 796995072 | bytes 7112704 | tf_op jit(solution)/shard_map/vd,td->vt/dot_general | solution.py:43
  116.8 73.0 %all-gather.7.cloned.1.call-done = bf16[768,5120]{1,0:T(8,128)(2,1)} async-done(((bf16[24,5120]{1,0:T(8,128)(2,1)}), bf16[768,5120]{1,0:T(8,128)(2,1)}) %all-gather.7.cloned.1.call-update) | async-done | bytes 7864336 | tf_op jit(solution)/shard_map/all_gather | solution.py:50
  189.8 5.4 %convolution_bitcast_fusion = f32[152,96,8]{0,2,1:T(8,128)S(1)} fusion(bf16[152,5120]{1,0:T(8,128)(2,1)S(1)} %copy-done, bf16[768,5120]{1,0:T(8,128)(2,1)} %all-gather.7.cloned.1.call-done), kind=kOutput, calls=%fused_computation.2 | convolution fusion | flops 1195376640 | bytes 9887744 | tf_op jit(solution)/shard_map/vd,td->vt/dot_general | solution.py:47
  195.3 0.6 gather_fusion
  195.9 0.2 fusion
  196.2 0.2 copy.22
  196.4 103.1 %all-reduce.1 = (f32[512]{0:T(512)S(1)}, f32[512]{0:T(512)S(1)}) all-reduce(f32[512]{0:T(512)S(1)} %reduce_max.22, f32[512]{0:T(512)S(1)} %get-tuple-element.9), channel_id=1, replica_groups=mesh['grp'=32,'vocab'=16] {'grp','vocab'}, use_global_device_ids=true, to_apply=%region_8.9 | all-reduce | flops 1024 | bytes 8192 | tf_op jit(solution)/shard_map/pmax | solution.py:58
  299.6 0.3 exponential_reduce_fusion
  299.9 0.1 reduce_sum.64
  300.0 0.1 multiply_reduce_fusion
  300.2 98.7 %all-reduce = (f32[512]{0:T(512)S(1)}, f32[512]{0:T(512)S(1)}, f32[512]{0:T(512)S(1)}) all-reduce(f32[512]{0:T(512)S(1)} %reduce_sum.64, f32[512]{0:T(512)S(1)} %get-tuple-element.3, f32[512]{0:T(512)S(1)} %get-tuple-element.2), channel_id=1, replica_groups=mesh['grp'=32,'vocab'=16] {'grp','vocab'}, use_global_device_ids=true, to_apply=%region_10.11 | all-reduce | flops 1536 | bytes 12288 | tf_op jit(solution)/shard_map/psum | solution.py:61
  398.9 0.6 dynamic_slice.3
  399.4 4.7 %convolution_convert_fusion = bf16[152,5120]{1,0:T(8,128)(2,1)} fusion(bf16[512,5120]{1,0:T(8,128)(2,1)} %all-gather.5.cloned.1.call-done, f32[152,512]{1,0:T(8,128)S(1)} %copy.22, f32[152,512]{1,0:T(8,128)S(1)} %get-tuple-element.10, f32[512]{0:T(512)S(1)} %get-tuple-element.4, f32[512]{0:T(512)S(1)} %get-tuple-element.7, f32[512]{0:T(512)S(1)} %get-tuple-element.5, ...), kind=kOutput, calls=%fused_computation.1 | convolution fusion | flops 798318592 | bytes 7432704 | tf_op jit(solution)/shard_map/dot_general | solution.py:75
  (21 shorter events, 0.7 us)
Async XLA Ops:
  7.2 182.7 %copy-start = (bf16[152,5120]{1,0:T(8,128)(2,1)S(1)}, bf16[152,5120]{1,0:T(8,128)(2,1)}, u32[]{:S(2)}) copy-start(bf16[152,5120]{1,0:T(8,128)(2,1)} %param.8) | copy-start | bytes 4669444
  7.2 104.7 %all-gather.5.cloned.1.call-start = ((), (), s32[]{:S(2)}) async-start(), calls=%async_computation | async-start | bytes 5406720 | tf_op jit(solution)/shard_map/all_gather | solution.py:42
  28.0 161.9 %all-gather.7.cloned.1.call-start = ((), (), s32[]{:S(2)}) async-start(), calls=%async_computation.1 | async-start | bytes 8110080 | tf_op jit(solution)/shard_map/all_gather | solution.py:50
Sparse Core Ops, SparseCore 0:
  28.1 83.7 all-gather.4
  114.6 75.1 all-gather.6
where the time goes:
time: 412 us; the launch traced here: 411 us
  blocking collectives  239 us (58%)
  waiting for transfers between devices  137 us (33%)
  matrix products  15 us (4%)
  between operations  14.2 us (3%)
  local copies, waits for them, and re-layouts  4.74 us (1%)
    pmax x1, blocking collectives, per_device(): lax.pmax((teacher_local, student_local), ('grp', 'vocab'))  103 us
    psum x1, blocking collectives, per_device(): lax.psum((jnp.sum(teacher_exp, axis=0), jnp.sum(student_exp, axis=0), jnp...  98.7 us
    all_gather x1, waiting for transfers between devices, per_device(): lax.all_gather(slot_cols, 'grp', axis=0, tiled=True)  73 us
    all_gather x1, waiting for transfers between devices, per_device(): student_all = lax.all_gather(student_cols, 'grp', axis=0, tiled=True)  63.4 us
    all_gather x1, blocking collectives, per_device(): student_cols = lax.all_gather(student_hidden, 'vocab', axis=1, tiled=True)  19.8 us
    all_gather x1, blocking collectives, per_device(): slot_cols = lax.all_gather(teacher_hidden, 'vocab', axis=1, tiled=True)  17.8 us
  transfers between devices with their start and end apart: 2, of which 2 were waited for; matrix products, arithmetic and copies ran while one was open for 2% of the time, Pallas kernels for 0%

commit v1 on v0

v1 whole, which is shorter than its diff:
```python
import jax
import jax.numpy as jnp
import numpy as np
from jax import lax
from jax.sharding import Mesh, PartitionSpec as P

TASKS = 8
NZ, NC, NX, NY = 16, 2, 4, 4
BLK = 8
SWAP = [(0, 1), (1, 0)]


def block_sources(route, groups, tasks, block_rows, total_tokens):
    flat_route = route.reshape(-1)
    block_count = 2 * groups
    block_ids = jnp.arange(block_count, dtype=jnp.int32)
    slot_ids = jnp.arange(flat_route.shape[0], dtype=jnp.int32)
    hits = flat_route[None, :] == block_ids[:, None]
    source = jnp.sum(jnp.where(hits, slot_ids[None, :], 0), axis=1)
    per_task = groups // tasks
    slot_task = slot_ids // route.shape[1] // per_task
    task_ids = jnp.arange(tasks, dtype=jnp.int32)
    alive = flat_route < block_count
    task_blocks = jnp.sum(
        jnp.where((slot_task[None, :] == task_ids[:, None]) & alive[None, :], 1, 0), axis=1
    ).astype(jnp.int32)
    source_task = source // route.shape[1] // per_task
    owning = jnp.sum(
        jnp.where(source_task[:, None] == task_ids[None, :], task_blocks[None, :], 0), axis=1
    )
    block_weight = total_tokens / (tasks * block_rows * owning.astype(jnp.float32))
    return source, block_weight


def spread(x, axes, n):
    return lax.all_to_all(jnp.broadcast_to(x[None], (n,) + x.shape), axes, 0, 0)


def ring_pieces(x, axis, n):
    me = lax.axis_index(axis)
    pieces = [x]
    for shift in range(1, n):
        pieces.append(lax.ppermute(x, axis, [(i, (i + shift) % n) for i in range(n)]))
    out = jnp.zeros((n,) + x.shape, x.dtype)
    for shift, piece in enumerate(pieces):
        out = lax.dynamic_update_index_in_dim(out, piece, (me - shift) % n, 0)
    return out


def merge(stats):
    top = jnp.max(stats[:, 0:2], axis=0)
    scale = jnp.exp(stats[:, 0:2] - top[None])
    total = jnp.sum(stats[:, 2:4] * scale, axis=0)
    cross = jnp.sum(stats[:, 4:5] * scale[:, 0:1], axis=0)
    return jnp.concatenate([top, total, cross, jnp.zeros((3, top.shape[1]), top.dtype)], axis=0)


def per_device(student_hidden, teacher_hidden, student_head, teacher_head, route):
    core = lax.axis_index("core")
    z = lax.axis_index("z")
    feats = student_hidden.shape[1]
    rows = student_head.shape[0]
    groups = NZ * NC
    half = NZ * BLK
    cols = 2 * half
    width = NX * NY * feats

    student_other = lax.ppermute(student_head, "core", SWAP)
    teacher_other = lax.ppermute(teacher_head, "core", SWAP)

    source, block_weight = block_sources(route, groups, TASKS, BLK, groups * 2 * BLK)
    zs = jnp.arange(NZ, dtype=jnp.int32)
    blocks = jnp.concatenate([2 * (2 * zs + core), 2 * (2 * zs + 1 - core) + 1])
    my_source = jnp.take(source, blocks)
    my_weight = jnp.repeat(jnp.take(block_weight, blocks), BLK)

    odd = lax.all_gather(student_hidden[BLK:], "core")
    odd = lax.dynamic_index_in_dim(odd, 1 - core, 0, keepdims=False)
    held = jnp.concatenate([student_hidden[:BLK], odd, teacher_hidden], axis=0)
    n_rows = held.shape[0]
    packed = jnp.concatenate(
        [
            held[:, :128],
            held[:, 128:256],
            jnp.concatenate([held[: n_rows // 2, 256:], held[n_rows // 2 :, 256:]], axis=1),
        ],
        axis=0,
    )
    got = spread(packed, "z", NZ)
    tail = got[:, 2 * n_rows :]
    slots = jnp.concatenate(
        [
            got[:, :n_rows],
            got[:, n_rows : 2 * n_rows],
            jnp.concatenate([tail[:, :, :64], tail[:, :, 64:]], axis=1),
        ],
        axis=2,
    ).reshape(NZ * n_rows, feats)
    inner = jnp.arange(BLK, dtype=jnp.int32)
    s_rows = (
        zs[None, :, None] * n_rows
        + jnp.arange(2, dtype=jnp.int32)[:, None, None] * BLK
        + inner[None, None, :]
    ).reshape(-1)
    t_first = (my_source // 3 // 2) * n_rows + 2 * BLK + (my_source % 3) * BLK
    t_rows = (t_first[:, None] + inner[None, :]).reshape(-1)
    pick = jnp.concatenate([s_rows, t_rows])
    onehot = (
        jnp.arange(NZ * n_rows, dtype=jnp.int32)[:, None] == pick[None, :]
    ).astype(jnp.bfloat16)
    placed = lax.dot_general(
        slots, onehot, (((0,), (0,)), ((), ())), preferred_element_type=jnp.float32
    ).astype(jnp.bfloat16)

    student_y = spread(placed[:, :cols], "y", NY)
    teacher_x = ring_pieces(placed[:, cols:], "x", NX)
    student_y, teacher_x = lax.optimization_barrier((student_y, teacher_x))
    student_t = spread(student_y, "x", NX).reshape(width, cols)
    teacher_yx = ring_pieces(teacher_x, "y", NY)
    teacher_t = jnp.swapaxes(teacher_yx, 0, 1).reshape(width, cols)

    student_partner = lax.ppermute(student_t, "core", SWAP)

    head_s = jnp.concatenate([student_head, student_other], axis=0)
    head_t = jnp.concatenate([teacher_head, teacher_other], axis=0)
    ls = jnp.dot(head_s, student_t, preferred_element_type=jnp.float32)
    lt = jnp.dot(head_t, teacher_t, preferred_element_type=jnp.float32)
    ms = jnp.max(ls, axis=0)
    mt = jnp.max(lt, axis=0)
    es = jnp.exp(ls - ms[None])
    et = jnp.exp(lt - mt[None])
    zero = jnp.zeros_like(ms)
    stats = jnp.stack(
        [mt, ms, jnp.sum(et, axis=0), jnp.sum(es, axis=0), jnp.sum(et * (lt - ls), axis=0), zero, zero, zero]
    )
    stats = merge(spread(stats, ("x", "y"), NX * NY))
    stats = merge(spread(stats, "z", NZ))
    lse = stats[0:2] + jnp.log(stats[2:4])
    token_loss = stats[4] / stats[2] - lse[0] + lse[1]
    grad = (
        my_weight[None] * (jnp.exp(ls - lse[1][None]) - jnp.exp(lt - lse[0][None]))
    ).astype(jnp.bfloat16)

    grad_in = lax.all_gather(grad[rows:], "core")
    grad_in = lax.dynamic_index_in_dim(grad_in, 1 - core, 0, keepdims=False)
    nt = (((1,), (1,)), ((), ()))
    head_grad = lax.dot_general(
        jnp.concatenate([grad[:rows], grad_in], axis=1),
        jnp.concatenate([student_t, student_partner], axis=1),
        nt,
        preferred_element_type=jnp.float32,
    ).astype(jnp.bfloat16)

    odd_loss = lax.all_gather(token_loss[half:], "core")
    odd_loss = lax.dynamic_index_in_dim(odd_loss, 1 - core, 0, keepdims=False)
    own_loss = jnp.concatenate(
        [
            lax.dynamic_slice_in_dim(token_loss, z * BLK, BLK, 0),
            lax.dynamic_slice_in_dim(odd_loss, z * BLK, BLK, 0),
        ]
    )
    return head_grad, own_loss


def solution(mesh):
    mesh = Mesh(np.asarray(mesh.devices).reshape(NZ, NC, NX, NY), ("z", "core", "x", "y"))
    grp, voc = ("z", "core"), ("x", "y")
    return jax.shard_map(
        per_device,
        mesh=mesh,
        in_specs=(P(grp, voc), P(grp, voc), P(grp + voc, None), P(grp + voc, None), P()),
        out_specs=(P(grp + voc, None), P(grp)),
        check_vma=False,
    )
```

time: 412 us -> 167 us (0.41)
  blocking collectives: 239 us -> 15.8 us
  waiting for transfers between devices: 137 us -> 51.4 us
  starting transfers between devices: 0.08 us -> 71.7 us
  between operations: 14.2 us -> 1.24 us
  local copies, waits for them, and re-layouts: 4.74 us -> 12.1 us
  matrix products: 15 us -> 10.5 us
    all_gather x2 -> x0, waiting for transfers between devices: 136 us -> none  [the longest x1 73 us: per_device(): lax.all_gather(slot_cols, 'grp', axis=0, tiled=True)]
    pmax x1 -> x0, blocking collectives: 103 us -> none  [per_device(): lax.pmax((teacher_local, student_local), ('grp', 'vocab'))]
    psum x1 -> x0, blocking collectives: 98.7 us -> none  [per_device(): lax.psum((jnp.sum(teacher_exp, axis=0), jnp.sum(student_exp, axis=0), jnp...]
    ppermute x0 -> x9, starting transfers between devices: none -> 36.6 us  [the longest x6 18.7 us: ring_pieces(): lax.ppermute(x, axis, [(i, (i + shift) % n) for i in range(n)])]
    all_to_all x0 -> x5, waiting for transfers between devices: none -> 35.7 us  [spread(): return lax.all_to_all(jnp.broadcast_to(x[None], (n,) + x.shape), axes, 0, 0)]
    all_to_all x0 -> x5, starting transfers between devices: none -> 35.1 us  [spread(): return lax.all_to_all(jnp.broadcast_to(x[None], (n,) + x.shape), axes, 0, 0)]
    all_gather x2 -> x3, blocking collectives: 37.6 us -> 15.8 us  [the longest x1 8.36 us: per_device(): odd = lax.all_gather(student_hidden[BLK:], 'core')]
    ppermute x0 -> x9, waiting for transfers between devices: none -> 15.6 us  [the longest x6 15.6 us: ring_pieces(): lax.ppermute(x, axis, [(i, (i + shift) % n) for i in range(n)])]
  transfers between devices with their start and end apart: 2 -> 14, of which waited for: 2 -> 6; matrix products, arithmetic and copies ran while one was open for 2% -> 8% of each run, Pallas kernels for 0% -> 0%
where the time goes in v1:
time: 167 us; the launch traced here: 166 us
  starting transfers between devices  71.7 us (43%)
  waiting for transfers between devices  51.4 us (31%)
  blocking collectives  15.8 us (9%)
  local copies, waits for them, and re-layouts  12.1 us (7%)
  matrix products  10.5 us (6%)
  other arithmetic  3.56 us (2%)
    all_to_all x5, waiting for transfers between devices, spread(): return lax.all_to_all(jnp.broadcast_to(x[None], (n,) + x.shape), axes, 0, 0)  35.7 us
    all_to_all x5, starting transfers between devices, spread(): return lax.all_to_all(jnp.broadcast_to(x[None], (n,) + x.shape), axes, 0, 0)  35.1 us
    ppermute x6, starting transfers between devices, ring_pieces(): lax.ppermute(x, axis, [(i, (i + shift) % n) for i in range(n)])  18.7 us
    ppermute x6, waiting for transfers between devices, ring_pieces(): lax.ppermute(x, axis, [(i, (i + shift) % n) for i in range(n)])  15.6 us
    ppermute x1, starting transfers between devices, per_device(): student_other = lax.ppermute(student_head, 'core', SWAP)  11.4 us
    all_gather x1, blocking collectives, per_device(): odd = lax.all_gather(student_hidden[BLK:], 'core')  8.36 us
    all_gather x1, blocking collectives, per_device(): odd_loss = lax.all_gather(token_loss[half:], 'core')  5.55 us
    broadcast_in_dim x5, local copies, waits for them, and re-layouts, spread(): return lax.all_to_all(jnp.broadcast_to(x[None], (n,) + x.shape), axes, 0, 0)  4.79 us
  transfers between devices with their start and end apart: 14, of which 6 were waited for; matrix products, arithmetic and copies ran while one was open for 8% of the time, Pallas kernels for 0%

profile of v1, /device:TPU:1, one launch (start us, length us, event | category | flops | bytes accessed | tf_op | source)
XLA Modules:
  0.0 166.3 jit_solution(4496094664249840678)
XLA Ops:
  1.3 8.4 %all-gather = bf16[16,320]{1,0:T(8,128)(2,1)S(1)} all-gather(bf16[8,320]{1,0:T(8,128)(2,1)S(1)} %get-tuple-element.26), channel_id=2, replica_groups=mesh['z'=16,'core'=2,'x'=4,'y'=4] {'core'}, dimensions={0}, use_global_device_ids=true | all-gather | bytes 15360 | tf_op jit(solution)/shard_map/all_gather | solution.py:77
  12.7 9.5 %all-to-all-start = ((bf16[16,100,128]{2,1,0:T(8,128)(2,1)}), bf16[16,100,128]{2,1,0:T(8,128)(2,1)S(1)}, u32[]{:S(2)}, u32[]{:S(2)}) async-start(bf16[16,100,128]{2,1,0:T(8,128)(2,1)} %broadcast_in_dim.139), calls=%async_computation | async-start | bytes 851968 | tf_op jit(solution)/shard_map/all_to_all | solution.py:36
  22.3 2.5 %collective-permute-start.4 = (bf16[152,5120]{1,0:T(8,128)(2,1)}, bf16[152,5120]{1,0:T(8,128)(2,1)}, u32[]{:S(2)}, u32[]{:S(2)}) collective-permute-start(bf16[152,5120]{1,0:T(8,128)(2,1)} %param.8), channel_id=1, source_target_pairs={{0,16},{16,0},{1,17},{17,1},{2,18},{18,2},{3,19},{19,3},{4,20},{20... | collective-permute-start | bytes 4669448 | tf_op jit(solution)/shard_map/ppermute | solution.py:69
  28.2 13.9 %all-to-all-done = bf16[16,100,128]{2,1,0:T(8,128)(2,1)S(1)} async-done(((bf16[16,100,128]{2,1,0:T(8,128)(2,1)}), bf16[16,100,128]{2,1,0:T(8,128)(2,1)S(1)}, u32[]{:S(2)}, u32[]{:S(2)}) %all-to-all-start) | async-done | bytes 409632 | tf_op jit(solution)/shard_map/all_to_all | solution.py:36
  42.8 3.1 %collective-permute-start.1 = (bf16[320,256]{1,0:T(8,128)(2,1)S(1)}, bf16[320,256]{1,0:T(8,128)(2,1)S(1)}, u32[]{:S(2)}, u32[]{:S(2)}) collective-permute-start(bf16[320,256]{1,0:T(8,128)(2,1)S(1)} %get-tuple-element.19), channel_id=1, source_target_pairs={{0,4},{4,8},{8,12},{12,0},{1,5},{5,9},{9,13},{13,1},{2,6},{6,10},{... | collective-permute-start | bytes 491528 | tf_op jit(solution)/shard_map/ppermute | solution.py:43
  46.0 4.4 %collective-permute-start.2 = (bf16[320,256]{1,0:T(8,128)(2,1)S(1)}, bf16[320,256]{1,0:T(8,128)(2,1)S(1)}, u32[]{:S(2)}, u32[]{:S(2)}) collective-permute-start(bf16[320,256]{1,0:T(8,128)(2,1)S(1)} %get-tuple-element.19), channel_id=1, source_target_pairs={{0,8},{4,12},{8,0},{12,4},{1,9},{5,13},{9,1},{13,5},{2,10},{6,14},... | collective-permute-start | bytes 491528 | tf_op jit(solution)/shard_map/ppermute | solution.py:43
  50.3 3.1 %collective-permute-start.3 = (bf16[320,256]{1,0:T(8,128)(2,1)S(1)}, bf16[320,256]{1,0:T(8,128)(2,1)S(1)}, u32[]{:S(2)}, u32[]{:S(2)}) collective-permute-start(bf16[320,256]{1,0:T(8,128)(2,1)S(1)} %get-tuple-element.19), channel_id=1, source_target_pairs={{0,12},{4,0},{8,4},{12,8},{1,13},{5,1},{9,5},{13,9},{2,14},{6,2},{... | collective-permute-start | bytes 491528 | tf_op jit(solution)/shard_map/ppermute | solution.py:43
  54.3 4.2 %all-to-all-start.1 = ((bf16[4,320,256]{2,1,0:T(8,128)(2,1)}), bf16[4,320,256]{2,1,0:T(8,128)(2,1)S(1)}, u32[]{:S(2)}, u32[]{:S(2)}) async-start(bf16[4,320,256]{2,1,0:T(8,128)(2,1)} %broadcast_in_dim.141), calls=%async_computation.1 | async-start | bytes 1310720 | tf_op jit(solution)/shard_map/all_to_all | solution.py:36
  58.6 7.5 %all-to-all-done.1 = bf16[4,320,256]{2,1,0:T(8,128)(2,1)S(1)} async-done(((bf16[4,320,256]{2,1,0:T(8,128)(2,1)}), bf16[4,320,256]{2,1,0:T(8,128)(2,1)S(1)}, u32[]{:S(2)}, u32[]{:S(2)}) %all-to-all-start.1) | async-done | bytes 655392 | tf_op jit(solution)/shard_map/all_to_all | solution.py:36
  67.9 3.7 %all-to-all-start.2 = ((bf16[4,4,320,256]{3,2,1,0:T(8,128)(2,1)}), bf16[4,4,320,256]{3,2,1,0:T(8,128)(2,1)S(1)}, u32[]{:S(2)}, u32[]{:S(2)}) async-start(bf16[4,4,320,256]{3,2,1,0:T(8,128)(2,1)} %broadcast_in_dim.147), calls=%async_computation.2 | async-start | bytes 5242880 | tf_op jit(solution)/shard_map/all_to_all | solution.py:36
  73.7 3.7 %collective-permute-start.6 = (bf16[4,320,256]{2,1,0:T(8,128)(2,1)S(1)}, bf16[4,320,256]{2,1,0:T(8,128)(2,1)}, u32[]{:S(2)}, u32[]{:S(2)}) collective-permute-start(bf16[4,320,256]{2,1,0:T(8,128)(2,1)S(1)} %bitcast_dynamic-update-slice_fusion.4), channel_id=1, source_target_pairs={{0,2},{1,3},{2,0},{3,1},{4,6},{5,7},{6,4},{7,5},{8,10},{9,11},{10,... | collective-permute-start | bytes 1966088 | tf_op jit(solution)/shard_map/ppermute | solution.py:43
  77.4 11.4 %collective-permute-start = (bf16[152,5120]{1,0:T(8,128)(2,1)}, bf16[152,5120]{1,0:T(8,128)(2,1)}, u32[]{:S(2)}, u32[]{:S(2)}) collective-permute-start(bf16[152,5120]{1,0:T(8,128)(2,1)} %param.7), channel_id=1, source_target_pairs={{0,16},{16,0},{1,17},{17,1},{2,18},{18,2},{3,19},{19,3},{4,20},{20... | collective-permute-start | bytes 4669448 | tf_op jit(solution)/shard_map/ppermute | solution.py:68
  88.9 2.2 %collective-permute-start.7 = (bf16[4,320,256]{2,1,0:T(8,128)(2,1)S(1)}, bf16[4,320,256]{2,1,0:T(8,128)(2,1)S(1)}, u32[]{:S(2)}, u32[]{:S(2)}) collective-permute-start(bf16[4,320,256]{2,1,0:T(8,128)(2,1)S(1)} %bitcast_dynamic-update-slice_fusion.4), channel_id=1, source_target_pairs={{0,3},{1,0},{2,1},{3,2},{4,7},{5,4},{6,5},{7,6},{8,11},{9,8},{10,9... | collective-permute-start | bytes 1966088 | tf_op jit(solution)/shard_map/ppermute | solution.py:43
  92.7 2.6 %collective-permute-done.6 = bf16[4,320,256]{2,1,0:T(8,128)(2,1)} collective-permute-done((bf16[4,320,256]{2,1,0:T(8,128)(2,1)S(1)}, bf16[4,320,256]{2,1,0:T(8,128)(2,1)}, u32[]{:S(2)}, u32[]{:S(2)}) %collective-permute-start.6) | collective-permute-done | bytes 655392 | tf_op jit(solution)/shard_map/ppermute | solution.py:43
  96.4 13.0 %collective-permute-done.7 = bf16[4,320,256]{2,1,0:T(8,128)(2,1)S(1)} collective-permute-done((bf16[4,320,256]{2,1,0:T(8,128)(2,1)S(1)}, bf16[4,320,256]{2,1,0:T(8,128)(2,1)S(1)}, u32[]{:S(2)}, u32[]{:S(2)}) %collective-permute-start.7) | collective-permute-done | bytes 655392 | tf_op jit(solution)/shard_map/ppermute | solution.py:43
  109.5 2.4 %fusion.41 = (f32[256]{0:T(256)S(1)}, f32[304,256]{1,0:T(8,128)S(1)}) fusion(bf16[5120,256]{1,0:T(8,128)(2,1)S(1)} %bitcast.58, bf16[152,5120]{1,0:T(8,128)(2,1)} %collective-permute-done.4, bf16[152,5120]{1,0:T(8,128)(2,1)S(1)} %copy-done), kind=kOutput, calls=%fused_computation.118 | convolution fusion | flops 803221248 | bytes 6046720 | tf_op jit(solution)/shard_map/dot_general | solution.py:127
  112.0 2.9 %fusion.42 = (f32[256]{0:T(256)S(1)}, f32[304,256]{1,0:T(8,128)S(1)}) fusion(bf16[5120,256]{1,0:T(8,128)(2,1)S(1)} %bitcast.55, bf16[152,5120]{1,0:T(8,128)(2,1)} %collective-permute-done, bf16[152,5120]{1,0:T(8,128)(2,1)} %param.7), kind=kOutput, calls=%fused_computation.119 | convolution fusion | flops 803221248 | bytes 6046720 | tf_op jit(solution)/shard_map/dot_general | solution.py:126
  115.7 7.7 %all-to-all-start.3 = ((f32[16,8,256]{2,1,0:T(8,128)}), f32[16,8,256]{2,1,0:T(8,128)S(1)}, u32[]{:S(2)}, u32[]{:S(2)}) async-start(f32[16,8,256]{2,1,0:T(8,128)} %broadcast_in_dim.153), calls=%async_computation.3 | async-start | bytes 262144 | tf_op jit(solution)/shard_map/all_to_all | solution.py:36
  123.5 6.6 %all-to-all-done.3 = f32[16,8,256]{2,1,0:T(8,128)S(1)} async-done(((f32[16,8,256]{2,1,0:T(8,128)}), f32[16,8,256]{2,1,0:T(8,128)S(1)}, u32[]{:S(2)}, u32[]{:S(2)}) %all-to-all-start.3) | async-done | bytes 131104 | tf_op jit(solution)/shard_map/all_to_all | solution.py:36
  131.0 10.0 %all-to-all-start.4 = ((f32[16,8,256]{2,1,0:T(8,128)}), f32[16,8,256]{2,1,0:T(8,128)S(1)}, u32[]{:S(2)}, u32[]{:S(2)}) async-start(f32[16,8,256]{2,1,0:T(8,128)} %broadcast_in_dim.155), calls=%async_computation.4 | async-start | bytes 262144 | tf_op jit(solution)/shard_map/all_to_all | solution.py:36
  141.0 4.0 %collective-permute-start.8 = (bf16[5120,256]{1,0:T(8,128)(2,1)S(1)}, bf16[5120,256]{1,0:T(8,128)(2,1)}, u32[]{:S(2)}, u32[]{:S(2)}) collective-permute-start(bf16[5120,256]{1,0:T(8,128)(2,1)S(1)} %bitcast.56), channel_id=1, source_target_pairs={{0,16},{16,0},{1,17},{17,1},{2,18},{18,2},{3,19},{19,3},{4,20},{20... | collective-permute-start | bytes 7864328 | tf_op jit(solution)/shard_map/ppermute | solution.py:122
  145.2 7.8 %all-to-all-done.4 = f32[16,8,256]{2,1,0:T(8,128)S(1)} async-done(((f32[16,8,256]{2,1,0:T(8,128)}), f32[16,8,256]{2,1,0:T(8,128)S(1)}, u32[]{:S(2)}, u32[]{:S(2)}) %all-to-all-start.4) | async-done | bytes 131104 | tf_op jit(solution)/shard_map/all_to_all | solution.py:36
  153.3 5.5 %all-gather.3 = f32[2,1,128]{2,1,0:T(1,128)S(1)} all-gather(f32[1,1,128]{2,1,0:T(1,128)S(1)} %slice_bitcast_fusion), channel_id=4, replica_groups=mesh['z'=16,'core'=2,'x'=4,'y'=4] {'core'}, dimensions={0}, use_global_device_ids=true | all-gather | bytes 1536 | tf_op jit(solution)/shard_map/all_gather | solution.py:154
  161.5 4.8 %convolution_convert_fusion = bf16[152,5120]{1,0:T(8,128)(2,1)} fusion(bf16[5120,256]{1,0:T(8,128)(2,1)} %collective-permute-done.8, bf16[5120,256]{1,0:T(8,128)(2,1)S(1)} %bitcast.57, bf16[152,256]{1,0:T(8,128)(2,1)S(1)} %dynamic-slice_bitcast_fusion, bf16[152,256]{1,0:T(8,128)(2,1)S(1)} %get-tuple-element.21), kind=kOutput, calls=%fused_computation.2 | convolution fusion | flops 808493056 | bytes 6955008 | tf_op jit(solution)/shard_map/dot_general | solution.py:147
  (89 shorter events, 20.3 us)
Async XLA Ops:
  12.7 29.4 %all-to-all-start = ((bf16[16,100,128]{2,1,0:T(8,128)(2,1)}), bf16[16,100,128]{2,1,0:T(8,128)(2,1)S(1)}, u32[]{:S(2)}, u32[]{:S(2)}) async-start(bf16[16,100,128]{2,1,0:T(8,128)(2,1)} %broadcast_in_dim.139), calls=%async_computation | async-start | bytes 851968 | tf_op jit(solution)/shard_map/all_to_all | solution.py:36
  22.3 87.2 %collective-permute-start.4 = (bf16[152,5120]{1,0:T(8,128)(2,1)}, bf16[152,5120]{1,0:T(8,128)(2,1)}, u32[]{:S(2)}, u32[]{:S(2)}) collective-permute-start(bf16[152,5120]{1,0:T(8,128)(2,1)} %param.8), channel_id=1, source_target_pairs={{0,16},{16,0},{1,17},{17,1},{2,18},{18,2},{3,19},{19,3},{4,20},{20... | collective-permute-start | bytes 4669448 | tf_op jit(solution)/shard_map/ppermute | solution.py:69
  42.8 15.7 %collective-permute-start.1 = (bf16[320,256]{1,0:T(8,128)(2,1)S(1)}, bf16[320,256]{1,0:T(8,128)(2,1)S(1)}, u32[]{:S(2)}, u32[]{:S(2)}) collective-permute-start(bf16[320,256]{1,0:T(8,128)(2,1)S(1)} %get-tuple-element.19), channel_id=1, source_target_pairs={{0,4},{4,8},{8,12},{12,0},{1,5},{5,9},{9,13},{13,1},{2,6},{6,10},{... | collective-permute-start | bytes 491528 | tf_op jit(solution)/shard_map/ppermute | solution.py:43
  46.0 12.6 %collective-permute-start.2 = (bf16[320,256]{1,0:T(8,128)(2,1)S(1)}, bf16[320,256]{1,0:T(8,128)(2,1)S(1)}, u32[]{:S(2)}, u32[]{:S(2)}) collective-permute-start(bf16[320,256]{1,0:T(8,128)(2,1)S(1)} %get-tuple-element.19), channel_id=1, source_target_pairs={{0,8},{4,12},{8,0},{12,4},{1,9},{5,13},{9,1},{13,5},{2,10},{6,14},... | collective-permute-start | bytes 491528 | tf_op jit(solution)/shard_map/ppermute | solution.py:43
  50.3 8.3 %collective-permute-start.3 = (bf16[320,256]{1,0:T(8,128)(2,1)S(1)}, bf16[320,256]{1,0:T(8,128)(2,1)S(1)}, u32[]{:S(2)}, u32[]{:S(2)}) collective-permute-start(bf16[320,256]{1,0:T(8,128)(2,1)S(1)} %get-tuple-element.19), channel_id=1, source_target_pairs={{0,12},{4,0},{8,4},{12,8},{1,13},{5,1},{9,5},{13,9},{2,14},{6,2},{... | collective-permute-start | bytes 491528 | tf_op jit(solution)/shard_map/ppermute | solution.py:43
  54.3 11.8 %all-to-all-start.1 = ((bf16[4,320,256]{2,1,0:T(8,128)(2,1)}), bf16[4,320,256]{2,1,0:T(8,128)(2,1)S(1)}, u32[]{:S(2)}, u32[]{:S(2)}) async-start(bf16[4,320,256]{2,1,0:T(8,128)(2,1)} %broadcast_in_dim.141), calls=%async_computation.1 | async-start | bytes 1310720 | tf_op jit(solution)/shard_map/all_to_all | solution.py:36
  67.9 44.1 %all-to-all-start.2 = ((bf16[4,4,320,256]{3,2,1,0:T(8,128)(2,1)}), bf16[4,4,320,256]{3,2,1,0:T(8,128)(2,1)S(1)}, u32[]{:S(2)}, u32[]{:S(2)}) async-start(bf16[4,4,320,256]{3,2,1,0:T(8,128)(2,1)} %broadcast_in_dim.147), calls=%async_computation.2 | async-start | bytes 5242880 | tf_op jit(solution)/shard_map/all_to_all | solution.py:36
  71.5 19.9 %collective-permute-start.5 = (bf16[4,320,256]{2,1,0:T(8,128)(2,1)S(1)}, bf16[4,320,256]{2,1,0:T(8,128)(2,1)}, u32[]{:S(2)}, u32[]{:S(2)}) collective-permute-start(bf16[4,320,256]{2,1,0:T(8,128)(2,1)S(1)} %bitcast_dynamic-update-slice_fusion.4), channel_id=1, source_target_pairs={{0,1},{1,2},{2,3},{3,0},{4,5},{5,6},{6,7},{7,4},{8,9},{9,10},{10,1... | collective-permute-start | bytes 1966088 | tf_op jit(solution)/shard_map/ppermute | solution.py:43
  73.7 21.6 %collective-permute-start.6 = (bf16[4,320,256]{2,1,0:T(8,128)(2,1)S(1)}, bf16[4,320,256]{2,1,0:T(8,128)(2,1)}, u32[]{:S(2)}, u32[]{:S(2)}) collective-permute-start(bf16[4,320,256]{2,1,0:T(8,128)(2,1)S(1)} %bitcast_dynamic-update-slice_fusion.4), channel_id=1, source_target_pairs={{0,2},{1,3},{2,0},{3,1},{4,6},{5,7},{6,4},{7,5},{8,10},{9,11},{10,... | collective-permute-start | bytes 1966088 | tf_op jit(solution)/shard_map/ppermute | solution.py:43
  77.4 34.5 %collective-permute-start = (bf16[152,5120]{1,0:T(8,128)(2,1)}, bf16[152,5120]{1,0:T(8,128)(2,1)}, u32[]{:S(2)}, u32[]{:S(2)}) collective-permute-start(bf16[152,5120]{1,0:T(8,128)(2,1)} %param.7), channel_id=1, source_target_pairs={{0,16},{16,0},{1,17},{17,1},{2,18},{18,2},{3,19},{19,3},{4,20},{20... | collective-permute-start | bytes 4669448 | tf_op jit(solution)/shard_map/ppermute | solution.py:68
  88.9 20.6 %collective-permute-start.7 = (bf16[4,320,256]{2,1,0:T(8,128)(2,1)S(1)}, bf16[4,320,256]{2,1,0:T(8,128)(2,1)S(1)}, u32[]{:S(2)}, u32[]{:S(2)}) collective-permute-start(bf16[4,320,256]{2,1,0:T(8,128)(2,1)S(1)} %bitcast_dynamic-update-slice_fusion.4), channel_id=1, source_target_pairs={{0,3},{1,0},{2,1},{3,2},{4,7},{5,4},{6,5},{7,6},{8,11},{9,8},{10,9... | collective-permute-start | bytes 1966088 | tf_op jit(solution)/shard_map/ppermute | solution.py:43
  91.4 18.1 %copy-start = (bf16[152,5120]{1,0:T(8,128)(2,1)S(1)}, bf16[152,5120]{1,0:T(8,128)(2,1)}, u32[]{:S(2)}) copy-start(bf16[152,5120]{1,0:T(8,128)(2,1)} %param.8) | copy-start | bytes 4669444
  115.7 14.4 %all-to-all-start.3 = ((f32[16,8,256]{2,1,0:T(8,128)}), f32[16,8,256]{2,1,0:T(8,128)S(1)}, u32[]{:S(2)}, u32[]{:S(2)}) async-start(f32[16,8,256]{2,1,0:T(8,128)} %broadcast_in_dim.153), calls=%async_computation.3 | async-start | bytes 262144 | tf_op jit(solution)/shard_map/all_to_all | solution.py:36
  131.0 22.0 %all-to-all-start.4 = ((f32[16,8,256]{2,1,0:T(8,128)}), f32[16,8,256]{2,1,0:T(8,128)S(1)}, u32[]{:S(2)}, u32[]{:S(2)}) async-start(f32[16,8,256]{2,1,0:T(8,128)} %broadcast_in_dim.155), calls=%async_computation.4 | async-start | bytes 262144 | tf_op jit(solution)/shard_map/all_to_all | solution.py:36
  141.0 20.5 %collective-permute-start.8 = (bf16[5120,256]{1,0:T(8,128)(2,1)S(1)}, bf16[5120,256]{1,0:T(8,128)(2,1)}, u32[]{:S(2)}, u32[]{:S(2)}) collective-permute-start(bf16[5120,256]{1,0:T(8,128)(2,1)S(1)} %bitcast.56), channel_id=1, source_target_pairs={{0,16},{16,0},{1,17},{17,1},{2,18},{18,2},{3,19},{19,3},{4,20},{20... | collective-permute-start | bytes 7864328 | tf_op jit(solution)/shard_map/ppermute | solution.py:122

commit v2 on v1

v2 whole, which is shorter than its diff:
```python
import functools

import jax
import jax.numpy as jnp
import numpy as np
from jax import lax
from jax.experimental import pallas as pl
from jax.experimental.pallas import tpu as pltpu
from jax.sharding import Mesh, PartitionSpec as P

TASKS = 8
NZ, NC, NX, NY = 16, 2, 4, 4
BLK = 8
SWAP = [(0, 1), (1, 0)]


def block_sources(route, groups, tasks, block_rows, total_tokens):
    flat_route = route.reshape(-1)
    block_count = 2 * groups
    block_ids = jnp.arange(block_count, dtype=jnp.int32)
    slot_ids = jnp.arange(flat_route.shape[0], dtype=jnp.int32)
    hits = flat_route[None, :] == block_ids[:, None]
    source = jnp.sum(jnp.where(hits, slot_ids[None, :], 0), axis=1)
    per_task = groups // tasks
    slot_task = slot_ids // route.shape[1] // per_task
    task_ids = jnp.arange(tasks, dtype=jnp.int32)
    alive = flat_route < block_count
    task_blocks = jnp.sum(
        jnp.where((slot_task[None, :] == task_ids[:, None]) & alive[None, :], 1, 0), axis=1
    ).astype(jnp.int32)
    source_task = source // route.shape[1] // per_task
    owning = jnp.sum(
        jnp.where(source_task[:, None] == task_ids[None, :], task_blocks[None, :], 0), axis=1
    )
    block_weight = total_tokens / (tasks * block_rows * owning.astype(jnp.float32))
    return source, block_weight


def spread(x, axes, n):
    return lax.all_to_all(jnp.broadcast_to(x[None], (n,) + x.shape), axes, 0, 0)


def merge(stats, t):
    top = jnp.max(stats[:, :, : 2 * t], axis=0)
    scale = jnp.exp(stats[:, :, : 2 * t] - top[None])
    total = jnp.sum(stats[:, :, 2 * t : 4 * t] * scale, axis=0)
    cross = jnp.sum(stats[:, :, 4 * t :] * scale[:, :, :t], axis=0)
    return jnp.concatenate([top, total, cross], axis=1)


LINES_X = [[x * NY + y for x in range(NX)] for y in range(NY)]
LINES_Y = [[x * NY + y for y in range(NY)] for x in range(NX)]


def by_core(first, second):
    return first + [[NX * NY + i for i in line] for line in second]


FIRST, LAST = by_core(LINES_X, LINES_Y), by_core(LINES_Y, LINES_X)


def spread_groups(x, axes, lines):
    copies = jnp.broadcast_to(x[None], (len(lines[0]),) + x.shape)
    return lax.all_to_all(copies, axes, 0, 0, axis_index_groups=lines)


def place_kernel(n, shifts, *refs):
    pieces, outs = refs[: 2 * n], refs[-2:]
    core = lax.axis_index("core")
    me = jnp.where(core == 0, lax.axis_index("y"), lax.axis_index("x"))
    for i, piece in enumerate(pieces):
        source = (me - shifts[i % n]) & (NX - 1)
        for j in range(NX):
            a = jnp.where(core == 0, j, source)
            b = jnp.where(core == 0, source, j)
            outs[i // n][a, b] = piece[j]


def place(pieces, shifts, shape, into=()):
    n = len(shifts)
    whole = pl.BlockSpec(memory_space=pltpu.VMEM)
    return pl.pallas_call(
        functools.partial(place_kernel, n, shifts),
        out_shape=(jax.ShapeDtypeStruct(shape, pieces[0].dtype),) * 2,
        in_specs=[whole] * (2 * n + len(into)),
        out_specs=(whole,) * 2,
        input_output_aliases={2 * n + i: i for i in range(len(into))},
        compiler_params=pltpu.CompilerParams(vmem_limit_bytes=20 * 1024 * 1024),
        name="place_blocks",
    )(*pieces, *(pltpu.with_memory_space_constraint(b, pltpu.VMEM) for b in into))


def per_device(student_hidden, teacher_hidden, student_head, teacher_head, route):
    core = lax.axis_index("core")
    x, y, z = lax.axis_index("x"), lax.axis_index("y"), lax.axis_index("z")
    feats = student_hidden.shape[1]
    rows = student_head.shape[0]
    groups = NZ * NC
    per_group = 2 * BLK
    half = NZ * BLK
    cols = 2 * half
    width = NX * NY * feats
    f32, bf16 = jnp.float32, jnp.bfloat16

    held = jnp.concatenate([student_hidden, teacher_hidden], axis=0)
    n_rows = held.shape[0]
    got = lax.all_gather(held, ("z", "core"))
    row = lax.broadcasted_iota(jnp.int32, (groups, n_rows), 1)
    group = lax.broadcasted_iota(jnp.int32, (groups, n_rows), 0)
    block = 2 * group + row // BLK
    for b in range(route.shape[1]):
        block = jnp.where((row - per_group) // BLK == b, route[:, b : b + 1], block)
    column = (block & 1) * half + (block >> 2) * BLK + row % BLK + jnp.where(row < per_group, 0, cols)
    mine = (block < 2 * groups) & (((block >> 1) & 1) == core)
    column = jnp.where(mine, column, -1)
    onehot = (column[:, :, None] == jnp.arange(2 * cols, dtype=jnp.int32)).astype(bf16)
    placed = lax.dot_general(
        got, onehot, (((0, 1), (0, 1)), ((), ())), preferred_element_type=f32
    ).astype(bf16)

    student_other = lax.ppermute(student_head, "core", SWAP)
    teacher_other = lax.ppermute(teacher_head, "core", SWAP)

    plane = ("core", "x", "y")
    both = jnp.stack([placed[:, :cols], placed[:, cols:]])
    once = spread_groups(both, plane, FIRST)
    student_1, teacher_1 = once[:, 0], once[:, 1]

    def pass_on(piece, k):
        return lax.ppermute(piece, plane, [(i[j], i[(j + k) % len(i)]) for i in LAST for j in range(len(i))])

    student_b, teacher_a = pass_on(student_1, 1), pass_on(teacher_1, 3)
    student_a, teacher_b = pass_on(student_1, 3), pass_on(teacher_1, 1)
    student_b, teacher_a, student_other, teacher_other = lax.optimization_barrier(
        (student_b, teacher_a, student_other, teacher_other)
    )
    student_c, teacher_c = pass_on(student_b, 1), pass_on(teacher_a, 3)
    shape = (NX, NY, feats, cols)
    student_t, teacher_t = place(
        (student_1, student_b, student_a, student_c, teacher_1, teacher_b, teacher_a, teacher_c),
        (0, 1, 3, 2),
        shape,
    )
    student_t, teacher_t = student_t.reshape(width, cols), teacher_t.reshape(width, cols)

    head_s = jnp.concatenate([student_head, student_other], axis=0)
    head_t = jnp.concatenate([teacher_head, teacher_other], axis=0)
    ls = jnp.dot(head_s, student_t, preferred_element_type=f32)
    lt = jnp.dot(head_t, teacher_t, preferred_element_type=f32)
    source, block_weight = block_sources(route, groups, TASKS, BLK, groups * per_group)
    my_weight = lax.dynamic_index_in_dim(block_weight.reshape(NZ, NC, 2), core, 1, keepdims=False)
    my_weight = jnp.repeat(my_weight.T.reshape(-1), BLK)
    ms = jnp.max(ls, axis=0)
    mt = jnp.max(lt, axis=0)
    es = jnp.exp(ls - ms[None])
    et = jnp.exp(lt - mt[None])
    stats = jnp.concatenate(
        [mt, ms, jnp.sum(et, axis=0), jnp.sum(es, axis=0), jnp.sum(et * (lt - ls), axis=0)]
    )[None]
    stats = merge(spread(stats, ("x", "y"), NX * NY), cols)
    stats, student_t = lax.optimization_barrier((stats, student_t))
    student_mate = lax.ppermute(student_t, "core", SWAP)
    stats = merge(spread(stats, "z", NZ), cols)[0]
    top_t, top_s, sum_t, sum_s = (stats[i * cols : (i + 1) * cols] for i in range(4))
    lse_t = top_t + jnp.log(sum_t)
    lse_s = top_s + jnp.log(sum_s)
    grad = (
        my_weight[None] * (jnp.exp(ls - lse_s[None]) - jnp.exp(lt - lse_t[None]))
    ).astype(bf16)

    grad_in = lax.all_gather(grad[rows:], "core")
    grad_in = lax.dynamic_index_in_dim(grad_in, 1 - core, 0, keepdims=False)
    nt = (((1,), (1,)), ((), ()))
    head_grad = lax.dot_general(
        jnp.concatenate([grad[:rows], grad_in], axis=1),
        jnp.concatenate([student_t, student_mate], axis=1),
        nt,
        preferred_element_type=f32,
    ).astype(bf16)
    own = lax.dynamic_index_in_dim(stats.reshape(10, NZ, BLK), z, 1, keepdims=False)
    own = own.reshape(5, per_group)
    loss = own[4] / own[2] - (own[0] + jnp.log(own[2])) + (own[1] + jnp.log(own[3]))
    return head_grad, loss


def solution(mesh):
    mesh = Mesh(np.asarray(mesh.devices).reshape(NZ, NC, NX, NY), ("z", "core", "x", "y"))
    grp, voc = ("z", "core"), ("x", "y")
    return jax.shard_map(
        per_device,
        mesh=mesh,
        in_specs=(P(grp, voc), P(grp, voc), P(grp + voc, None), P(grp + voc, None), P()),
        out_specs=(P(grp + voc, None), P(grp)),
        check_vma=False,
    )
```

time: 167 us -> 147 us (0.88)
  blocking collectives: 15.8 us -> 43.9 us
  starting transfers between devices: 71.7 us -> 44.9 us
  waiting for transfers between devices: 51.4 us -> 35.9 us
  local copies, waits for them, and re-layouts: 12.1 us -> 4.83 us
  Pallas kernels: 0 us -> 1.84 us
  other arithmetic: 3.56 us -> 1.82 us
    all_gather x2 -> x1, blocking collectives: 13.9 us -> 40.2 us  [per_device(): got = lax.all_gather(held, ('z', 'core'))]
    all_to_all x5 -> x2, starting transfers between devices: 35.1 us -> 11.3 us  [spread(): return lax.all_to_all(jnp.broadcast_to(x[None], (n,) + x.shape), axes, 0, 0)]
    all_to_all x5 -> x2, waiting for transfers between devices: 35.7 us -> 17.7 us  [spread(): return lax.all_to_all(jnp.broadcast_to(x[None], (n,) + x.shape), axes, 0, 0)]
    ppermute x1, starting transfers between devices: 11.4 us -> 2.16 us  [per_device(): student_other = lax.ppermute(student_head, 'core', SWAP)]
    all_to_all x0 -> x1, waiting for transfers between devices: none -> 7.11 us  [spread_groups(): return lax.all_to_all(copies, axes, 0, 0, axis_index_groups=lines)]
    ppermute x7, waiting for transfers between devices: 15.6 us -> 11 us  [the longest x6 11 us: pass_on(): lax.ppermute(piece, plane, [(i[j], i[(j + k) % len(i)]) for i in LAST for...]
    all_to_all x0 -> x1, starting transfers between devices: none -> 4.19 us  [spread_groups(): return lax.all_to_all(copies, axes, 0, 0, axis_index_groups=lines)]
    broadcast_in_dim x5 -> x2, local copies, waits for them, and re-layouts: 4.79 us -> 1.36 us  [spread(): return lax.all_to_all(jnp.broadcast_to(x[None], (n,) + x.shape), axes, 0, 0)]
  transfers between devices with their start and end apart: 14 -> 12, of which waited for: 6 -> 8; matrix products, arithmetic and copies ran while one was open for 8% -> 2% of each run, Pallas kernels for 0% -> 0%
where the time goes in v2:
time: 147 us; the launch traced here: 146 us
  starting transfers between devices  44.9 us (31%)
  blocking collectives  43.9 us (30%)
  waiting for transfers between devices  35.9 us (24%)
  matrix products  11.5 us (8%)
  local copies, waits for them, and re-layouts  4.83 us (3%)
  Pallas kernels  1.84 us (1%)
  other arithmetic  1.82 us (1%)
    all_gather x1, blocking collectives, per_device(): got = lax.all_gather(held, ('z', 'core'))  40.2 us
    ppermute x6, starting transfers between devices, pass_on(): lax.ppermute(piece, plane, [(i[j], i[(j + k) % len(i)]) for i in LAST for...  18.3 us
    all_to_all x2, waiting for transfers between devices, spread(): return lax.all_to_all(jnp.broadcast_to(x[None], (n,) + x.shape), axes, 0, 0)  17.7 us
    all_to_all x2, starting transfers between devices, spread(): return lax.all_to_all(jnp.broadcast_to(x[None], (n,) + x.shape), axes, 0, 0)  11.3 us
    ppermute x6, waiting for transfers between devices, pass_on(): lax.ppermute(piece, plane, [(i[j], i[(j + k) % len(i)]) for i in LAST for...  11 us
    all_to_all x1, waiting for transfers between devices, spread_groups(): return lax.all_to_all(copies, axes, 0, 0, axis_index_groups=lines)  7.11 us
    ppermute x1, starting transfers between devices, per_device(): student_mate = lax.ppermute(student_t, 'core', SWAP)  6.81 us
    dot_general x1, matrix products, per_device(): lax.dot_general(jnp.concatenate([grad[:rows], grad_in], axis=1), jnp.conc...  4.74 us
  transfers between devices with their start and end apart: 12, of which 8 were waited for; matrix products, arithmetic and copies ran while one was open for 2% of the time, Pallas kernels for 0%

profile of v2, /device:TPU:1, one launch (start us, length us, event | category | flops | bytes accessed | tf_op | source)
XLA Modules:
  0.0 145.8 jit_solution(13763827116172499965)
XLA Ops:
  2.3 40.2 %all-gather = bf16[1280,320]{1,0:T(8,128)(2,1)S(1)} all-gather(bf16[40,320]{1,0:T(8,128)(2,1)S(1)} %pad_maximum_fusion.1), channel_id=2, replica_groups=mesh['z'=16,'core'=2,'x'=4,'y'=4] {'z','core'}, dimensions={0}, use_global_device_ids=true | all-gather | bytes 844800 | tf_op jit(solution)/shard_map/all_gather | solution.py:107
  43.5 1.1 broadcast_in_dim.110
  44.6 4.2 %all-to-all-start = ((bf16[4,2,320,256]{3,2,1,0:T(8,128)(2,1)}), bf16[4,2,320,256]{3,2,1,0:T(8,128)(2,1)S(1)}, u32[]{:S(2)}, u32[]{:S(2)}) async-start(bf16[4,2,320,256]{3,2,1,0:T(8,128)(2,1)} %broadcast_in_dim.110), calls=%async_computation | async-start | bytes 2621440 | tf_op jit(solution)/shard_map/all_to_all | solution.py:64
  48.8 2.2 %collective-permute-start.2 = (bf16[152,5120]{1,0:T(8,128)(2,1)}, bf16[152,5120]{1,0:T(8,128)(2,1)}, u32[]{:S(2)}, u32[]{:S(2)}) collective-permute-start(bf16[152,5120]{1,0:T(8,128)(2,1)} %param.7), channel_id=1, source_target_pairs={{0,16},{16,0},{1,17},{17,1},{2,18},{18,2},{3,19},{19,3},{4,20},{20... | collective-permute-start | bytes 4669448 | tf_op jit(solution)/shard_map/ppermute | solution.py:121
  51.0 2.2 %collective-permute-start.3 = (bf16[152,5120]{1,0:T(8,128)(2,1)}, bf16[152,5120]{1,0:T(8,128)(2,1)}, u32[]{:S(2)}, u32[]{:S(2)}) collective-permute-start(bf16[152,5120]{1,0:T(8,128)(2,1)} %param.8), channel_id=1, source_target_pairs={{0,16},{16,0},{1,17},{17,1},{2,18},{18,2},{3,19},{19,3},{4,20},{20... | collective-permute-start | bytes 4669448 | tf_op jit(solution)/shard_map/ppermute | solution.py:122
  53.2 7.1 %all-to-all-done = bf16[4,2,320,256]{3,2,1,0:T(8,128)(2,1)S(1)} async-done(((bf16[4,2,320,256]{3,2,1,0:T(8,128)(2,1)}), bf16[4,2,320,256]{3,2,1,0:T(8,128)(2,1)S(1)}, u32[]{:S(2)}, u32[]{:S(2)}) %all-to-all-start) | async-done | bytes 1310752 | tf_op jit(solution)/shard_map/all_to_all | solution.py:64
  60.4 2.8 %collective-permute-start = (bf16[4,320,256]{2,1,0:T(8,128)(2,1)S(1)}, bf16[4,320,256]{2,1,0:T(8,128)(2,1)S(1)}, u32[]{:S(2)}, u32[]{:S(2)}) collective-permute-start(bf16[4,320,256]{2,1,0:T(8,128)(2,1)S(1)} %get-tuple-element.26.refs_0_), channel_id=1, source_target_pairs={{0,1},{1,2},{2,3},{3,0},{4,5},{5,6},{6,7},{7,4},{8,9},{9,10},{10,1... | collective-permute-start | bytes 1966088 | tf_op jit(solution)/shard_map/ppermute | solution.py:130
  63.2 3.7 %collective-permute-start.1 = (bf16[4,320,256]{2,1,0:T(8,128)(2,1)S(1)}, bf16[4,320,256]{2,1,0:T(8,128)(2,1)S(1)}, u32[]{:S(2)}, u32[]{:S(2)}) collective-permute-start(bf16[4,320,256]{2,1,0:T(8,128)(2,1)S(1)} %get-tuple-element.25.refs_4_), channel_id=1, source_target_pairs={{0,3},{1,0},{2,1},{3,2},{4,7},{5,4},{6,5},{7,6},{8,11},{9,8},{10,9... | collective-permute-start | bytes 1966088 | tf_op jit(solution)/shard_map/ppermute | solution.py:130
  66.9 2.9 %collective-permute-start.4 = (bf16[4,320,256]{2,1,0:T(8,128)(2,1)S(1)}, bf16[4,320,256]{2,1,0:T(8,128)(2,1)S(1)}, u32[]{:S(2)}, u32[]{:S(2)}) collective-permute-start(bf16[4,320,256]{2,1,0:T(8,128)(2,1)S(1)} %get-tuple-element.26.refs_0_), channel_id=1, source_target_pairs={{0,3},{1,0},{2,1},{3,2},{4,7},{5,4},{6,5},{7,6},{8,11},{9,8},{10,9... | collective-permute-start | bytes 1966088 | tf_op jit(solution)/shard_map/ppermute | solution.py:130
  69.8 2.4 %collective-permute-start.6 = (bf16[4,320,256]{2,1,0:T(8,128)(2,1)S(1)}, bf16[4,320,256]{2,1,0:T(8,128)(2,1)}, u32[]{:S(2)}, u32[]{:S(2)}) collective-permute-start(bf16[4,320,256]{2,1,0:T(8,128)(2,1)S(1)} %get-tuple-element.25.refs_4_), channel_id=1, source_target_pairs={{0,1},{1,2},{2,3},{3,0},{4,5},{5,6},{6,7},{7,4},{8,9},{9,10},{10,1... | collective-permute-start | bytes 1966088 | tf_op jit(solution)/shard_map/ppermute | solution.py:130
  73.2 1.6 %collective-permute-done.1.refs_6_ = bf16[4,320,256]{2,1,0:T(8,128)(2,1)S(1)} collective-permute-done((bf16[4,320,256]{2,1,0:T(8,128)(2,1)S(1)}, bf16[4,320,256]{2,1,0:T(8,128)(2,1)S(1)}, u32[]{:S(2)}, u32[]{:S(2)}) %collective-permute-start.1) | collective-permute-done | bytes 655392 | tf_op jit(solution)/shard_map/ppermute | solution.py:130
  74.8 3.1 %collective-permute-start.5 = (bf16[4,320,256]{2,1,0:T(8,128)(2,1)S(1)}, bf16[4,320,256]{2,1,0:T(8,128)(2,1)}, u32[]{:S(2)}, u32[]{:S(2)}) collective-permute-start(bf16[4,320,256]{2,1,0:T(8,128)(2,1)S(1)} %collective-permute-done.refs_1_), channel_id=1, source_target_pairs={{0,1},{1,2},{2,3},{3,0},{4,5},{5,6},{6,7},{7,4},{8,9},{9,10},{10,1... | collective-permute-start | bytes 1966088 | tf_op jit(solution)/shard_map/ppermute | solution.py:130
  77.9 3.4 %collective-permute-start.7 = (bf16[4,320,256]{2,1,0:T(8,128)(2,1)S(1)}, bf16[4,320,256]{2,1,0:T(8,128)(2,1)}, u32[]{:S(2)}, u32[]{:S(2)}) collective-permute-start(bf16[4,320,256]{2,1,0:T(8,128)(2,1)S(1)} %collective-permute-done.1.refs_6_), channel_id=1, source_target_pairs={{0,3},{1,0},{2,1},{3,2},{4,7},{5,4},{6,5},{7,6},{8,11},{9,8},{10,9... | collective-permute-start | bytes 1966088 | tf_op jit(solution)/shard_map/ppermute | solution.py:130
  82.7 7.0 %collective-permute-done.5.refs_3_ = bf16[4,320,256]{2,1,0:T(8,128)(2,1)} collective-permute-done((bf16[4,320,256]{2,1,0:T(8,128)(2,1)S(1)}, bf16[4,320,256]{2,1,0:T(8,128)(2,1)}, u32[]{:S(2)}, u32[]{:S(2)}) %collective-permute-start.5) | collective-permute-done | bytes 655392 | tf_op jit(solution)/shard_map/ppermute | solution.py:130
  89.7 1.8 %place_blocks.1 = (bf16[4,4,320,256]{3,2,1,0:T(8,128)(2,1)S(1)}, bf16[4,4,320,256]{3,2,1,0:T(8,128)(2,1)S(1)}) custom-call(bf16[4,320,256]{2,1,0:T(8,128)(2,1)S(1)} %get-tuple-element.26.refs_0_, bf16[4,320,256]{2,1,0:T(8,128)(2,1)S(1)} %collective-permute-done.refs_1_, bf16[4,320,256]{2,1,0:T(8,128)(2,1)S(1)} %collective-permute-done.4.refs_2_, ...), custom_call_target="tpu_custom_call" | custom-call | tf_op jit(solution)/shard_map/place_blocks/pallas_call | solution.py:82
  91.6 3.4 %fusion.45 = (f32[256]{0:T(256)S(1)}, f32[304,256]{1,0:T(8,128)S(1)}) fusion(bf16[5120,256]{1,0:T(8,128)(2,1)S(1)} %bitcast.42, bf16[152,5120]{1,0:T(8,128)(2,1)} %collective-permute-done.2, bf16[152,5120]{1,0:T(8,128)(2,1)S(1)} %copy-done.3), kind=kOutput, calls=%fused_computation.124 | convolution fusion | flops 803221248 | bytes 6046720 | tf_op jit(solution)/shard_map/dot_general | solution.py:148
  95.0 2.6 %fusion.44 = (f32[256]{0:T(256)S(1)}, f32[304,256]{1,0:T(8,128)S(1)}) fusion(bf16[5120,256]{1,0:T(8,128)(2,1)S(1)} %bitcast.45, bf16[152,5120]{1,0:T(8,128)(2,1)} %collective-permute-done.3, bf16[152,5120]{1,0:T(8,128)(2,1)S(1)} %copy-done.4), kind=kOutput, calls=%fused_computation.123 | convolution fusion | flops 803221248 | bytes 6046720 | tf_op jit(solution)/shard_map/dot_general | solution.py:149
  98.5 4.9 %all-to-all-start.1 = ((f32[16,1,1280]{2,1,0:T(1,128)}), f32[16,1,1280]{2,1,0:T(1,128)S(1)}, u32[]{:S(2)}, u32[]{:S(2)}) async-start(f32[16,1,1280]{2,1,0:T(1,128)} %broadcast_in_dim.111), calls=%async_computation.1 | async-start | bytes 163840 | tf_op jit(solution)/shard_map/all_to_all | solution.py:40
  103.6 6.3 %all-to-all-done.1 = f32[16,1,1280]{2,1,0:T(1,128)S(1)} async-done(((f32[16,1,1280]{2,1,0:T(1,128)}), f32[16,1,1280]{2,1,0:T(1,128)S(1)}, u32[]{:S(2)}, u32[]{:S(2)}) %all-to-all-start.1) | async-done | bytes 81952 | tf_op jit(solution)/shard_map/all_to_all | solution.py:40
  110.0 6.8 %collective-permute-start.8 = (bf16[5120,256]{1,0:T(8,128)(2,1)S(1)}, bf16[5120,256]{1,0:T(8,128)(2,1)}, u32[]{:S(2)}, u32[]{:S(2)}) collective-permute-start(bf16[5120,256]{1,0:T(8,128)(2,1)S(1)} %bitcast.43), channel_id=1, source_target_pairs={{0,16},{16,0},{1,17},{17,1},{2,18},{18,2},{3,19},{19,3},{4,20},{20... | collective-permute-start | bytes 7864328 | tf_op jit(solution)/shard_map/ppermute | solution.py:162
  117.9 6.4 %all-to-all-start.2 = ((f32[16,1,1280]{2,1,0:T(1,128)}), f32[16,1,1280]{2,1,0:T(1,128)S(1)}, u32[]{:S(2)}, u32[]{:S(2)}) async-start(f32[16,1,1280]{2,1,0:T(1,128)} %broadcast_in_dim.113), calls=%async_computation.2 | async-start | bytes 163840 | tf_op jit(solution)/shard_map/all_to_all | solution.py:40
  124.9 11.4 %all-to-all-done.2 = f32[16,1,1280]{2,1,0:T(1,128)S(1)} async-done(((f32[16,1,1280]{2,1,0:T(1,128)}), f32[16,1,1280]{2,1,0:T(1,128)S(1)}, u32[]{:S(2)}, u32[]{:S(2)}) %all-to-all-start.2) | async-done | bytes 81952 | tf_op jit(solution)/shard_map/all_to_all | solution.py:40
  137.3 3.7 %all-gather.1 = bf16[304,256]{1,0:T(8,128)(2,1)S(1)} all-gather(bf16[152,256]{1,0:T(8,128)(2,1)S(1)} %get-tuple-element.30), channel_id=3, replica_groups=mesh['z'=16,'core'=2,'x'=4,'y'=4] {'core'}, dimensions={0}, use_global_device_ids=true | all-gather | bytes 233472 | tf_op jit(solution)/shard_map/all_gather | solution.py:171
  141.0 4.7 %convolution_convert_fusion = bf16[152,5120]{1,0:T(8,128)(2,1)} fusion(bf16[5120,256]{1,0:T(8,128)(2,1)} %collective-permute-done.8, bf16[5120,256]{1,0:T(8,128)(2,1)S(1)} %bitcast.44, bf16[152,256]{1,0:T(8,128)(2,1)S(1)} %dynamic-slice_bitcast_fusion, bf16[152,256]{1,0:T(8,128)(2,1)S(1)} %get-tuple-element.29), kind=kOutput, calls=%fused_computation | convolution fusion | flops 808493056 | bytes 6955008 | tf_op jit(solution)/shard_map/dot_general | solution.py:174
  (73 shorter events, 8.7 us)
Async XLA Ops:
  44.6 15.6 %all-to-all-start = ((bf16[4,2,320,256]{3,2,1,0:T(8,128)(2,1)}), bf16[4,2,320,256]{3,2,1,0:T(8,128)(2,1)S(1)}, u32[]{:S(2)}, u32[]{:S(2)}) async-start(bf16[4,2,320,256]{3,2,1,0:T(8,128)(2,1)} %broadcast_in_dim.110), calls=%async_computation | async-start | bytes 2621440 | tf_op jit(solution)/shard_map/all_to_all | solution.py:64
  48.8 20.9 %collective-permute-start.2 = (bf16[152,5120]{1,0:T(8,128)(2,1)}, bf16[152,5120]{1,0:T(8,128)(2,1)}, u32[]{:S(2)}, u32[]{:S(2)}) collective-permute-start(bf16[152,5120]{1,0:T(8,128)(2,1)} %param.7), channel_id=1, source_target_pairs={{0,16},{16,0},{1,17},{17,1},{2,18},{18,2},{3,19},{19,3},{4,20},{20... | collective-permute-start | bytes 4669448 | tf_op jit(solution)/shard_map/ppermute | solution.py:121
  51.0 21.2 %collective-permute-start.3 = (bf16[152,5120]{1,0:T(8,128)(2,1)}, bf16[152,5120]{1,0:T(8,128)(2,1)}, u32[]{:S(2)}, u32[]{:S(2)}) collective-permute-start(bf16[152,5120]{1,0:T(8,128)(2,1)} %param.8), channel_id=1, source_target_pairs={{0,16},{16,0},{1,17},{17,1},{2,18},{18,2},{3,19},{19,3},{4,20},{20... | collective-permute-start | bytes 4669448 | tf_op jit(solution)/shard_map/ppermute | solution.py:122
  60.4 12.8 %collective-permute-start = (bf16[4,320,256]{2,1,0:T(8,128)(2,1)S(1)}, bf16[4,320,256]{2,1,0:T(8,128)(2,1)S(1)}, u32[]{:S(2)}, u32[]{:S(2)}) collective-permute-start(bf16[4,320,256]{2,1,0:T(8,128)(2,1)S(1)} %get-tuple-element.26.refs_0_), channel_id=1, source_target_pairs={{0,1},{1,2},{2,3},{3,0},{4,5},{5,6},{6,7},{7,4},{8,9},{9,10},{10,1... | collective-permute-start | bytes 1966088 | tf_op jit(solution)/shard_map/ppermute | solution.py:130
  63.2 11.6 %collective-permute-start.1 = (bf16[4,320,256]{2,1,0:T(8,128)(2,1)S(1)}, bf16[4,320,256]{2,1,0:T(8,128)(2,1)S(1)}, u32[]{:S(2)}, u32[]{:S(2)}) collective-permute-start(bf16[4,320,256]{2,1,0:T(8,128)(2,1)S(1)} %get-tuple-element.25.refs_4_), channel_id=1, source_target_pairs={{0,3},{1,0},{2,1},{3,2},{4,7},{5,4},{6,5},{7,6},{8,11},{9,8},{10,9... | collective-permute-start | bytes 1966088 | tf_op jit(solution)/shard_map/ppermute | solution.py:130
  66.9 15.1 %collective-permute-start.4 = (bf16[4,320,256]{2,1,0:T(8,128)(2,1)S(1)}, bf16[4,320,256]{2,1,0:T(8,128)(2,1)S(1)}, u32[]{:S(2)}, u32[]{:S(2)}) collective-permute-start(bf16[4,320,256]{2,1,0:T(8,128)(2,1)S(1)} %get-tuple-element.26.refs_0_), channel_id=1, source_target_pairs={{0,3},{1,0},{2,1},{3,2},{4,7},{5,4},{6,5},{7,6},{8,11},{9,8},{10,9... | collective-permute-start | bytes 1966088 | tf_op jit(solution)/shard_map/ppermute | solution.py:130
  69.8 12.9 %collective-permute-start.6 = (bf16[4,320,256]{2,1,0:T(8,128)(2,1)S(1)}, bf16[4,320,256]{2,1,0:T(8,128)(2,1)}, u32[]{:S(2)}, u32[]{:S(2)}) collective-permute-start(bf16[4,320,256]{2,1,0:T(8,128)(2,1)S(1)} %get-tuple-element.25.refs_4_), channel_id=1, source_target_pairs={{0,1},{1,2},{2,3},{3,0},{4,5},{5,6},{6,7},{7,4},{8,9},{9,10},{10,1... | collective-permute-start | bytes 1966088 | tf_op jit(solution)/shard_map/ppermute | solution.py:130
  74.8 14.9 %collective-permute-start.5 = (bf16[4,320,256]{2,1,0:T(8,128)(2,1)S(1)}, bf16[4,320,256]{2,1,0:T(8,128)(2,1)}, u32[]{:S(2)}, u32[]{:S(2)}) collective-permute-start(bf16[4,320,256]{2,1,0:T(8,128)(2,1)S(1)} %collective-permute-done.refs_1_), channel_id=1, source_target_pairs={{0,1},{1,2},{2,3},{3,0},{4,5},{5,6},{6,7},{7,4},{8,9},{9,10},{10,1... | collective-permute-start | bytes 1966088 | tf_op jit(solution)/shard_map/ppermute | solution.py:130
  77.9 11.8 %collective-permute-start.7 = (bf16[4,320,256]{2,1,0:T(8,128)(2,1)S(1)}, bf16[4,320,256]{2,1,0:T(8,128)(2,1)}, u32[]{:S(2)}, u32[]{:S(2)}) collective-permute-start(bf16[4,320,256]{2,1,0:T(8,128)(2,1)S(1)} %collective-permute-done.1.refs_6_), channel_id=1, source_target_pairs={{0,3},{1,0},{2,1},{3,2},{4,7},{5,4},{6,5},{7,6},{8,11},{9,8},{10,9... | collective-permute-start | bytes 1966088 | tf_op jit(solution)/shard_map/ppermute | solution.py:130
  81.3 10.3 %copy-start.3 = (bf16[152,5120]{1,0:T(8,128)(2,1)S(1)}, bf16[152,5120]{1,0:T(8,128)(2,1)}, u32[]{:S(2)}) copy-start(bf16[152,5120]{1,0:T(8,128)(2,1)} %param.7) | copy-start | bytes 4669444
  91.6 3.4 %copy-start = (bf16[4,4,320,256]{3,2,1,0:T(8,128)(2,1)}, bf16[4,4,320,256]{3,2,1,0:T(8,128)(2,1)S(1)}, u32[]{:S(2)}) copy-start(bf16[4,4,320,256]{3,2,1,0:T(8,128)(2,1)S(1)} %get-tuple-element.13) | copy-start | bytes 7864324
  91.6 3.4 %copy-start.4 = (bf16[152,5120]{1,0:T(8,128)(2,1)S(1)}, bf16[152,5120]{1,0:T(8,128)(2,1)}, u32[]{:S(2)}) copy-start(bf16[152,5120]{1,0:T(8,128)(2,1)} %param.8) | copy-start | bytes 4669444
  95.0 8.4 %copy-start.2 = (s32[32,3]{0,1:T(4,128)S(1)}, s32[32,3]{0,1:T(4,128)}, u32[]{:S(2)}) copy-start(s32[32,3]{0,1:T(4,128)} %param.9) | copy-start | bytes 1156
  95.0 15.0 %copy-start.1 = (bf16[4,4,320,256]{3,2,1,0:T(8,128)(2,1)S(1)}, bf16[4,4,320,256]{3,2,1,0:T(8,128)(2,1)}, u32[]{:S(2)}) copy-start(bf16[4,4,320,256]{3,2,1,0:T(8,128)(2,1)} %copy-done) | copy-start | bytes 7864324
  98.5 11.4 %all-to-all-start.1 = ((f32[16,1,1280]{2,1,0:T(1,128)}), f32[16,1,1280]{2,1,0:T(1,128)S(1)}, u32[]{:S(2)}, u32[]{:S(2)}) async-start(f32[16,1,1280]{2,1,0:T(1,128)} %broadcast_in_dim.111), calls=%async_computation.1 | async-start | bytes 163840 | tf_op jit(solution)/shard_map/all_to_all | solution.py:40
  110.0 31.0 %collective-permute-start.8 = (bf16[5120,256]{1,0:T(8,128)(2,1)S(1)}, bf16[5120,256]{1,0:T(8,128)(2,1)}, u32[]{:S(2)}, u32[]{:S(2)}) collective-permute-start(bf16[5120,256]{1,0:T(8,128)(2,1)S(1)} %bitcast.43), channel_id=1, source_target_pairs={{0,16},{16,0},{1,17},{17,1},{2,18},{18,2},{3,19},{19,3},{4,20},{20... | collective-permute-start | bytes 7864328 | tf_op jit(solution)/shard_map/ppermute | solution.py:162
  117.9 18.3 %all-to-all-start.2 = ((f32[16,1,1280]{2,1,0:T(1,128)}), f32[16,1,1280]{2,1,0:T(1,128)S(1)}, u32[]{:S(2)}, u32[]{:S(2)}) async-start(f32[16,1,1280]{2,1,0:T(1,128)} %broadcast_in_dim.113), calls=%async_computation.2 | async-start | bytes 163840 | tf_op jit(solution)/shard_map/all_to_all | solution.py:40

commit v3 on v2

--- a/solution.py
+++ b/solution.py
@@ -43,9 +43,9 @@
 def merge(stats, t):
     top = jnp.max(stats[:, :, : 2 * t], axis=0)
     scale = jnp.exp(stats[:, :, : 2 * t] - top[None])
-    total = jnp.sum(stats[:, :, 2 * t : 4 * t] * scale, axis=0)
-    cross = jnp.sum(stats[:, :, 4 * t :] * scale[:, :, :t], axis=0)
-    return jnp.concatenate([top, total, cross], axis=1)
+    total = jnp.sum(scale, axis=0)
+    mean = jnp.sum(stats[:, :, 2 * t :] * scale[:, :, :t], axis=0) / total[:, :t]
+    return jnp.concatenate([top + jnp.log(total), mean], axis=1)
 
 
 LINES_X = [[x * NY + y for x in range(NX)] for y in range(NY)]
@@ -64,28 +64,29 @@
     return lax.all_to_all(copies, axes, 0, 0, axis_index_groups=lines)
 
 
-def place_kernel(n, shifts, *refs):
-    pieces, outs = refs[: 2 * n], refs[-2:]
+def place_kernel(shifts, *refs):
+    out = refs[-1]
     core = lax.axis_index("core")
     me = jnp.where(core == 0, lax.axis_index("y"), lax.axis_index("x"))
-    for i, piece in enumerate(pieces):
-        source = (me - shifts[i % n]) & (NX - 1)
+    for piece, shift in zip(refs, shifts):
+        source = (me - shift) & (NX - 1)
         for j in range(NX):
             a = jnp.where(core == 0, j, source)
             b = jnp.where(core == 0, source, j)
-            outs[i // n][a, b] = piece[j]
+            out[a, b] = piece[j]
 
 
-def place(pieces, shifts, shape, into=()):
-    n = len(shifts)
+def place(pieces, shifts, into=()):
+    n = len(pieces)
     whole = pl.BlockSpec(memory_space=pltpu.VMEM)
+    shape = (NX, NY) + pieces[0].shape[1:]
     return pl.pallas_call(
-        functools.partial(place_kernel, n, shifts),
-        out_shape=(jax.ShapeDtypeStruct(shape, pieces[0].dtype),) * 2,
-        in_specs=[whole] * (2 * n + len(into)),
-        out_specs=(whole,) * 2,
-        input_output_aliases={2 * n + i: i for i in range(len(into))},
-        compiler_params=pltpu.CompilerParams(vmem_limit_bytes=20 * 1024 * 1024),
+        functools.partial(place_kernel, shifts),
+        out_shape=jax.ShapeDtypeStruct(shape, pieces[0].dtype),
+        in_specs=[whole] * (n + len(into)),
+        out_specs=whole,
+        input_output_aliases={n: 0} if into else {},
+        compiler_params=pltpu.CompilerParams(vmem_limit_bytes=8 * 1024 * 1024),
         name="place_blocks",
     )(*pieces, *(pltpu.with_memory_space_constraint(b, pltpu.VMEM) for b in into))
 
@@ -135,13 +136,12 @@
         (student_b, teacher_a, student_other, teacher_other)
     )
     student_c, teacher_c = pass_on(student_b, 1), pass_on(teacher_a, 3)
-    shape = (NX, NY, feats, cols)
-    student_t, teacher_t = place(
-        (student_1, student_b, student_a, student_c, teacher_1, teacher_b, teacher_a, teacher_c),
-        (0, 1, 3, 2),
-        shape,
-    )
-    student_t, teacher_t = student_t.reshape(width, cols), teacher_t.reshape(width, cols)
+    near_s = place((student_1, student_b, student_a), (0, 1, 3))
+    near_t = place((teacher_1, teacher_b, teacher_a), (0, 1, 3))
+    student_t = place((student_c,), (2,), (near_s,)).reshape(width, cols)
+    teacher_t = place((teacher_c,), (2,), (near_t,)).reshape(width, cols)
+
+    student_mate = lax.ppermute(student_t, "core", SWAP)
 
     head_s = jnp.concatenate([student_head, student_other], axis=0)
     head_t = jnp.concatenate([teacher_head, teacher_other], axis=0)
@@ -154,16 +154,12 @@
     mt = jnp.max(lt, axis=0)
     es = jnp.exp(ls - ms[None])
     et = jnp.exp(lt - mt[None])
-    stats = jnp.concatenate(
-        [mt, ms, jnp.sum(et, axis=0), jnp.sum(es, axis=0), jnp.sum(et * (lt - ls), axis=0)]
-    )[None]
+    total_s, total_t = jnp.sum(es, axis=0), jnp.sum(et, axis=0)
+    mean = jnp.sum(et * (lt - ls), axis=0) / total_t
+    stats = jnp.concatenate([mt + jnp.log(total_t), ms + jnp.log(total_s), mean])[None]
     stats = merge(spread(stats, ("x", "y"), NX * NY), cols)
-    stats, student_t = lax.optimization_barrier((stats, student_t))
-    student_mate = lax.ppermute(student_t, "core", SWAP)
     stats = merge(spread(stats, "z", NZ), cols)[0]
-    top_t, top_s, sum_t, sum_s = (stats[i * cols : (i + 1) * cols] for i in range(4))
-    lse_t = top_t + jnp.log(sum_t)
-    lse_s = top_s + jnp.log(sum_s)
+    lse_t, lse_s = stats[:cols], stats[cols : 2 * cols]
     grad = (
         my_weight[None] * (jnp.exp(ls - lse_s[None]) - jnp.exp(lt - lse_t[None]))
     ).astype(bf16)
@@ -177,9 +173,9 @@
         nt,
         preferred_element_type=f32,
     ).astype(bf16)
-    own = lax.dynamic_index_in_dim(stats.reshape(10, NZ, BLK), z, 1, keepdims=False)
-    own = own.reshape(5, per_group)
-    loss = own[4] / own[2] - (own[0] + jnp.log(own[2])) + (own[1] + jnp.log(own[3]))
+    own = lax.dynamic_index_in_dim(stats.reshape(6, NZ, BLK), z, 1, keepdims=False)
+    own = own.reshape(3, per_group)
+    loss = own[2] - own[0] + own[1]
     return head_grad, loss
 
 

time: 147 us -> 140 us (0.952)
  waiting for transfers between devices: 35.9 us -> 26.5 us
  blocking collectives: 43.9 us -> 47.2 us
    all_to_all x2, waiting for transfers between devices: 17.7 us -> 12.7 us  [spread(): return lax.all_to_all(jnp.broadcast_to(x[None], (n,) + x.shape), axes, 0, 0)]
    ppermute x6, waiting for transfers between devices: 11 us -> 6.71 us  [pass_on(): lax.ppermute(piece, plane, [(i[j], i[(j + k) % len(i)]) for i in LAST for...]
    all_gather x1, blocking collectives: 3.69 us -> 6.96 us  [per_device(): grad_in = lax.all_gather(grad[rows:], 'core')]
    ppermute x1, starting transfers between devices: 6.81 us -> 4.87 us  [per_device(): student_mate = lax.ppermute(student_t, 'core', SWAP)]
  transfers between devices with their start and end apart: 12 -> 12, of which waited for: 8 -> 6; matrix products, arithmetic and copies ran while one was open for 2% -> 4% of each run, Pallas kernels for 0% -> 2%
where the time goes in v3:
time: 140 us; the launch traced here: 139 us
  blocking collectives  47.2 us (34%)
  starting transfers between devices  43.6 us (31%)
  waiting for transfers between devices  26.5 us (19%)
  matrix products  11.3 us (8%)
  local copies, waits for them, and re-layouts  4.7 us (3%)
  Pallas kernels  2.59 us (2%)
  other arithmetic  1.82 us (1%)
    all_gather x1, blocking collectives, per_device(): got = lax.all_gather(held, ('z', 'core'))  40.2 us
    ppermute x6, starting transfers between devices, pass_on(): lax.ppermute(piece, plane, [(i[j], i[(j + k) % len(i)]) for i in LAST for...  19.7 us
    all_to_all x2, waiting for transfers between devices, spread(): return lax.all_to_all(jnp.broadcast_to(x[None], (n,) + x.shape), axes, 0, 0)  12.7 us
    all_to_all x2, starting transfers between devices, spread(): return lax.all_to_all(jnp.broadcast_to(x[None], (n,) + x.shape), axes, 0, 0)  10.5 us
    all_to_all x1, waiting for transfers between devices, spread_groups(): return lax.all_to_all(copies, axes, 0, 0, axis_index_groups=lines)  7.11 us
    all_gather x1, blocking collectives, per_device(): grad_in = lax.all_gather(grad[rows:], 'core')  6.96 us
    ppermute x6, waiting for transfers between devices, pass_on(): lax.ppermute(piece, plane, [(i[j], i[(j + k) % len(i)]) for i in LAST for...  6.71 us
    ppermute x1, starting transfers between devices, per_device(): student_mate = lax.ppermute(student_t, 'core', SWAP)  4.87 us
  transfers between devices with their start and end apart: 12, of which 6 were waited for; matrix products, arithmetic and copies ran while one was open for 4% of the time, Pallas kernels for 2%

profile of v3, /device:TPU:1, one launch (start us, length us, event | category | flops | bytes accessed | tf_op | source)
XLA Modules:
  0.0 138.8 jit_solution(1181253163899142335)
XLA Ops:
  2.3 40.2 %all-gather = bf16[1280,320]{1,0:T(8,128)(2,1)S(1)} all-gather(bf16[40,320]{1,0:T(8,128)(2,1)S(1)} %pad_maximum_fusion.1), channel_id=2, replica_groups=mesh['z'=16,'core'=2,'x'=4,'y'=4] {'z','core'}, dimensions={0}, use_global_device_ids=true | all-gather | bytes 844800 | tf_op jit(solution)/shard_map/all_gather | solution.py:108
  44.6 4.3 %all-to-all-start = ((bf16[4,2,320,256]{3,2,1,0:T(8,128)(2,1)}), bf16[4,2,320,256]{3,2,1,0:T(8,128)(2,1)S(1)}, u32[]{:S(2)}, u32[]{:S(2)}) async-start(bf16[4,2,320,256]{3,2,1,0:T(8,128)(2,1)} %broadcast_in_dim.110), calls=%async_computation | async-start | bytes 2621440 | tf_op jit(solution)/shard_map/all_to_all | solution.py:64
  49.0 2.2 %collective-permute-start.2 = (bf16[152,5120]{1,0:T(8,128)(2,1)}, bf16[152,5120]{1,0:T(8,128)(2,1)}, u32[]{:S(2)}, u32[]{:S(2)}) collective-permute-start(bf16[152,5120]{1,0:T(8,128)(2,1)} %param.7), channel_id=1, source_target_pairs={{0,16},{16,0},{1,17},{17,1},{2,18},{18,2},{3,19},{19,3},{4,20},{20... | collective-permute-start | bytes 4669448 | tf_op jit(solution)/shard_map/ppermute | solution.py:122
  51.1 2.2 %collective-permute-start.3 = (bf16[152,5120]{1,0:T(8,128)(2,1)}, bf16[152,5120]{1,0:T(8,128)(2,1)}, u32[]{:S(2)}, u32[]{:S(2)}) collective-permute-start(bf16[152,5120]{1,0:T(8,128)(2,1)} %param.8), channel_id=1, source_target_pairs={{0,16},{16,0},{1,17},{17,1},{2,18},{18,2},{3,19},{19,3},{4,20},{20... | collective-permute-start | bytes 4669448 | tf_op jit(solution)/shard_map/ppermute | solution.py:123
  53.3 7.1 %all-to-all-done = bf16[4,2,320,256]{3,2,1,0:T(8,128)(2,1)S(1)} async-done(((bf16[4,2,320,256]{3,2,1,0:T(8,128)(2,1)}), bf16[4,2,320,256]{3,2,1,0:T(8,128)(2,1)S(1)}, u32[]{:S(2)}, u32[]{:S(2)}) %all-to-all-start) | async-done | bytes 1310752 | tf_op jit(solution)/shard_map/all_to_all | solution.py:64
  60.5 2.8 %collective-permute-start = (bf16[4,320,256]{2,1,0:T(8,128)(2,1)S(1)}, bf16[4,320,256]{2,1,0:T(8,128)(2,1)}, u32[]{:S(2)}, u32[]{:S(2)}) collective-permute-start(bf16[4,320,256]{2,1,0:T(8,128)(2,1)S(1)} %get-tuple-element.18.refs_0_), channel_id=1, source_target_pairs={{0,1},{1,2},{2,3},{3,0},{4,5},{5,6},{6,7},{7,4},{8,9},{9,10},{10,1... | collective-permute-start | bytes 1966088 | tf_op jit(solution)/shard_map/ppermute | solution.py:131
  63.3 3.7 %collective-permute-start.1 = (bf16[4,320,256]{2,1,0:T(8,128)(2,1)S(1)}, bf16[4,320,256]{2,1,0:T(8,128)(2,1)}, u32[]{:S(2)}, u32[]{:S(2)}) collective-permute-start(bf16[4,320,256]{2,1,0:T(8,128)(2,1)S(1)} %get-tuple-element.17.refs_0_), channel_id=1, source_target_pairs={{0,3},{1,0},{2,1},{3,2},{4,7},{5,4},{6,5},{7,6},{8,11},{9,8},{10,9... | collective-permute-start | bytes 1966088 | tf_op jit(solution)/shard_map/ppermute | solution.py:131
  67.3 1.9 %collective-permute-start.7 = (bf16[4,320,256]{2,1,0:T(8,128)(2,1)S(1)}, bf16[4,320,256]{2,1,0:T(8,128)(2,1)S(1)}, u32[]{:S(2)}, u32[]{:S(2)}) collective-permute-start(bf16[4,320,256]{2,1,0:T(8,128)(2,1)S(1)} %get-tuple-element.17.refs_0_), channel_id=1, source_target_pairs={{0,1},{1,2},{2,3},{3,0},{4,5},{5,6},{6,7},{7,4},{8,9},{9,10},{10,1... | collective-permute-start | bytes 1966088 | tf_op jit(solution)/shard_map/ppermute | solution.py:131
  69.3 4.6 %collective-permute-start.5 = (bf16[4,320,256]{2,1,0:T(8,128)(2,1)S(1)}, bf16[4,320,256]{2,1,0:T(8,128)(2,1)S(1)}, u32[]{:S(2)}, u32[]{:S(2)}) collective-permute-start(bf16[4,320,256]{2,1,0:T(8,128)(2,1)S(1)} %get-tuple-element.18.refs_0_), channel_id=1, source_target_pairs={{0,3},{1,0},{2,1},{3,2},{4,7},{5,4},{6,5},{7,6},{8,11},{9,8},{10,9... | collective-permute-start | bytes 1966088 | tf_op jit(solution)/shard_map/ppermute | solution.py:131
  73.9 1.2 collective-permute-done.1.refs_2_
  75.0 4.8 %collective-permute-start.6 = (bf16[4,320,256]{2,1,0:T(8,128)(2,1)}, bf16[4,320,256]{2,1,0:T(8,128)(2,1)S(1)}, u32[]{:S(2)}, u32[]{:S(2)}) collective-permute-start(bf16[4,320,256]{2,1,0:T(8,128)(2,1)} %collective-permute-done.1.refs_2_), channel_id=1, source_target_pairs={{0,3},{1,0},{2,1},{3,2},{4,7},{5,4},{6,5},{7,6},{8,11},{9,8},{10,9... | collective-permute-start | bytes 1966088 | tf_op jit(solution)/shard_map/ppermute | solution.py:131
  79.9 1.9 %collective-permute-start.4 = (bf16[4,320,256]{2,1,0:T(8,128)(2,1)}, bf16[4,320,256]{2,1,0:T(8,128)(2,1)S(1)}, u32[]{:S(2)}, u32[]{:S(2)}) collective-permute-start(bf16[4,320,256]{2,1,0:T(8,128)(2,1)} %collective-permute-done.refs_1_), channel_id=1, source_target_pairs={{0,1},{1,2},{2,3},{3,0},{4,5},{5,6},{6,7},{7,4},{8,9},{9,10},{10,1... | collective-permute-start | bytes 1966088 | tf_op jit(solution)/shard_map/ppermute | solution.py:131
  81.9 1.2 place_blocks.6.refs_1_
  83.2 1.2 place_blocks.4.refs_1_
  84.4 4.6 %collective-permute-done.6.refs_0_ = bf16[4,320,256]{2,1,0:T(8,128)(2,1)S(1)} collective-permute-done((bf16[4,320,256]{2,1,0:T(8,128)(2,1)}, bf16[4,320,256]{2,1,0:T(8,128)(2,1)S(1)}, u32[]{:S(2)}, u32[]{:S(2)}) %collective-permute-start.6) | collective-permute-done | bytes 655392 | tf_op jit(solution)/shard_map/ppermute | solution.py:131
  89.1 2.9 %fusion.39 = (f32[256]{0:T(256)S(1)}, f32[304,256]{1,0:T(8,128)S(1)}) fusion(bf16[5120,256]{1,0:T(8,128)(2,1)S(1)} %bitcast.45, bf16[152,5120]{1,0:T(8,128)(2,1)} %collective-permute-done.3, bf16[152,5120]{1,0:T(8,128)(2,1)} %param.8), kind=kOutput, calls=%fused_computation.114 | convolution fusion | flops 803221248 | bytes 6046720 | tf_op jit(solution)/shard_map/dot_general | solution.py:149
  93.0 2.9 %fusion.40 = (f32[256]{0:T(256)S(1)}, f32[304,256]{1,0:T(8,128)S(1)}) fusion(bf16[5120,256]{1,0:T(8,128)(2,1)S(1)} %bitcast.42, bf16[152,5120]{1,0:T(8,128)(2,1)} %collective-permute-done.2, bf16[152,5120]{1,0:T(8,128)(2,1)} %param.7), kind=kOutput, calls=%fused_computation.115 | convolution fusion | flops 803221248 | bytes 6046720 | tf_op jit(solution)/shard_map/dot_general | solution.py:148
  96.7 4.0 %all-to-all-start.1 = ((f32[16,1,768]{2,1,0:T(1,128)}), f32[16,1,768]{2,1,0:T(1,128)S(1)}, u32[]{:S(2)}, u32[]{:S(2)}) async-start(f32[16,1,768]{2,1,0:T(1,128)} %broadcast_in_dim.111), calls=%async_computation.1 | async-start | bytes 98304 | tf_op jit(solution)/shard_map/all_to_all | solution.py:40
  100.8 4.9 %collective-permute-start.8 = (bf16[5120,256]{1,0:T(8,128)(2,1)S(1)}, bf16[5120,256]{1,0:T(8,128)(2,1)}, u32[]{:S(2)}, u32[]{:S(2)}) collective-permute-start(bf16[5120,256]{1,0:T(8,128)(2,1)S(1)} %bitcast.43), channel_id=1, source_target_pairs={{0,16},{16,0},{1,17},{17,1},{2,18},{18,2},{3,19},{19,3},{4,20},{20... | collective-permute-start | bytes 7864328 | tf_op jit(solution)/shard_map/ppermute | solution.py:144
  105.6 1.5 %all-to-all-done.1 = f32[16,1,768]{2,1,0:T(1,128)S(1)} async-done(((f32[16,1,768]{2,1,0:T(1,128)}), f32[16,1,768]{2,1,0:T(1,128)S(1)}, u32[]{:S(2)}, u32[]{:S(2)}) %all-to-all-start.1) | async-done | bytes 49184 | tf_op jit(solution)/shard_map/all_to_all | solution.py:40
  108.0 6.4 %all-to-all-start.2 = ((f32[16,1,768]{2,1,0:T(1,128)}), f32[16,1,768]{2,1,0:T(1,128)S(1)}, u32[]{:S(2)}, u32[]{:S(2)}) async-start(f32[16,1,768]{2,1,0:T(1,128)} %broadcast_in_dim.113), calls=%async_computation.2 | async-start | bytes 98304 | tf_op jit(solution)/shard_map/all_to_all | solution.py:40
  114.9 11.1 %all-to-all-done.2 = f32[16,1,768]{2,1,0:T(1,128)S(1)} async-done(((f32[16,1,768]{2,1,0:T(1,128)}), f32[16,1,768]{2,1,0:T(1,128)S(1)}, u32[]{:S(2)}, u32[]{:S(2)}) %all-to-all-start.2) | async-done | bytes 49184 | tf_op jit(solution)/shard_map/all_to_all | solution.py:40
  127.1 7.0 %all-gather.1 = bf16[304,256]{1,0:T(8,128)(2,1)S(1)} all-gather(bf16[152,256]{1,0:T(8,128)(2,1)S(1)} %get-tuple-element.22), channel_id=3, replica_groups=mesh['z'=16,'core'=2,'x'=4,'y'=4] {'core'}, dimensions={0}, use_global_device_ids=true | all-gather | bytes 233472 | tf_op jit(solution)/shard_map/all_gather | solution.py:167
  134.0 4.7 %convolution_convert_fusion = bf16[152,5120]{1,0:T(8,128)(2,1)} fusion(bf16[5120,256]{1,0:T(8,128)(2,1)} %collective-permute-done.8, bf16[5120,256]{1,0:T(8,128)(2,1)S(1)} %bitcast.44, bf16[152,256]{1,0:T(8,128)(2,1)S(1)} %dynamic-slice_bitcast_fusion, bf16[152,256]{1,0:T(8,128)(2,1)S(1)} %get-tuple-element.21), kind=kOutput, calls=%fused_computation | convolution fusion | flops 808493056 | bytes 6955008 | tf_op jit(solution)/shard_map/dot_general | solution.py:170
  (68 shorter events, 8.4 us)
Async XLA Ops:
  44.6 22.4 %copy-start = (s32[32,3]{0,1:T(4,128)S(1)}, s32[32,3]{0,1:T(4,128)}, u32[]{:S(2)}) copy-start(s32[32,3]{0,1:T(4,128)} %param.9) | copy-start | bytes 1156
  44.6 15.8 %all-to-all-start = ((bf16[4,2,320,256]{3,2,1,0:T(8,128)(2,1)}), bf16[4,2,320,256]{3,2,1,0:T(8,128)(2,1)S(1)}, u32[]{:S(2)}, u32[]{:S(2)}) async-start(bf16[4,2,320,256]{3,2,1,0:T(8,128)(2,1)} %broadcast_in_dim.110), calls=%async_computation | async-start | bytes 2621440 | tf_op jit(solution)/shard_map/all_to_all | solution.py:64
  49.0 20.3 %collective-permute-start.2 = (bf16[152,5120]{1,0:T(8,128)(2,1)}, bf16[152,5120]{1,0:T(8,128)(2,1)}, u32[]{:S(2)}, u32[]{:S(2)}) collective-permute-start(bf16[152,5120]{1,0:T(8,128)(2,1)} %param.7), channel_id=1, source_target_pairs={{0,16},{16,0},{1,17},{17,1},{2,18},{18,2},{3,19},{19,3},{4,20},{20... | collective-permute-start | bytes 4669448 | tf_op jit(solution)/shard_map/ppermute | solution.py:122
  51.1 22.7 %collective-permute-start.3 = (bf16[152,5120]{1,0:T(8,128)(2,1)}, bf16[152,5120]{1,0:T(8,128)(2,1)}, u32[]{:S(2)}, u32[]{:S(2)}) collective-permute-start(bf16[152,5120]{1,0:T(8,128)(2,1)} %param.8), channel_id=1, source_target_pairs={{0,16},{16,0},{1,17},{17,1},{2,18},{18,2},{3,19},{19,3},{4,20},{20... | collective-permute-start | bytes 4669448 | tf_op jit(solution)/shard_map/ppermute | solution.py:123
  60.5 13.4 %collective-permute-start = (bf16[4,320,256]{2,1,0:T(8,128)(2,1)S(1)}, bf16[4,320,256]{2,1,0:T(8,128)(2,1)}, u32[]{:S(2)}, u32[]{:S(2)}) collective-permute-start(bf16[4,320,256]{2,1,0:T(8,128)(2,1)S(1)} %get-tuple-element.18.refs_0_), channel_id=1, source_target_pairs={{0,1},{1,2},{2,3},{3,0},{4,5},{5,6},{6,7},{7,4},{8,9},{9,10},{10,1... | collective-permute-start | bytes 1966088 | tf_op jit(solution)/shard_map/ppermute | solution.py:131
  63.3 11.7 %collective-permute-start.1 = (bf16[4,320,256]{2,1,0:T(8,128)(2,1)S(1)}, bf16[4,320,256]{2,1,0:T(8,128)(2,1)}, u32[]{:S(2)}, u32[]{:S(2)}) collective-permute-start(bf16[4,320,256]{2,1,0:T(8,128)(2,1)S(1)} %get-tuple-element.17.refs_0_), channel_id=1, source_target_pairs={{0,3},{1,0},{2,1},{3,2},{4,7},{5,4},{6,5},{7,6},{8,11},{9,8},{10,9... | collective-permute-start | bytes 1966088 | tf_op jit(solution)/shard_map/ppermute | solution.py:131
  67.3 14.6 %collective-permute-start.7 = (bf16[4,320,256]{2,1,0:T(8,128)(2,1)S(1)}, bf16[4,320,256]{2,1,0:T(8,128)(2,1)S(1)}, u32[]{:S(2)}, u32[]{:S(2)}) collective-permute-start(bf16[4,320,256]{2,1,0:T(8,128)(2,1)S(1)} %get-tuple-element.17.refs_0_), channel_id=1, source_target_pairs={{0,1},{1,2},{2,3},{3,0},{4,5},{5,6},{6,7},{7,4},{8,9},{9,10},{10,1... | collective-permute-start | bytes 1966088 | tf_op jit(solution)/shard_map/ppermute | solution.py:131
  69.3 13.9 %collective-permute-start.5 = (bf16[4,320,256]{2,1,0:T(8,128)(2,1)S(1)}, bf16[4,320,256]{2,1,0:T(8,128)(2,1)S(1)}, u32[]{:S(2)}, u32[]{:S(2)}) collective-permute-start(bf16[4,320,256]{2,1,0:T(8,128)(2,1)S(1)} %get-tuple-element.18.refs_0_), channel_id=1, source_target_pairs={{0,3},{1,0},{2,1},{3,2},{4,7},{5,4},{6,5},{7,6},{8,11},{9,8},{10,9... | collective-permute-start | bytes 1966088 | tf_op jit(solution)/shard_map/ppermute | solution.py:131
  75.0 13.9 %collective-permute-start.6 = (bf16[4,320,256]{2,1,0:T(8,128)(2,1)}, bf16[4,320,256]{2,1,0:T(8,128)(2,1)S(1)}, u32[]{:S(2)}, u32[]{:S(2)}) collective-permute-start(bf16[4,320,256]{2,1,0:T(8,128)(2,1)} %collective-permute-done.1.refs_2_), channel_id=1, source_target_pairs={{0,3},{1,0},{2,1},{3,2},{4,7},{5,4},{6,5},{7,6},{8,11},{9,8},{10,9... | collective-permute-start | bytes 1966088 | tf_op jit(solution)/shard_map/ppermute | solution.py:131
  79.9 13.0 %collective-permute-start.4 = (bf16[4,320,256]{2,1,0:T(8,128)(2,1)}, bf16[4,320,256]{2,1,0:T(8,128)(2,1)S(1)}, u32[]{:S(2)}, u32[]{:S(2)}) collective-permute-start(bf16[4,320,256]{2,1,0:T(8,128)(2,1)} %collective-permute-done.refs_1_), channel_id=1, source_target_pairs={{0,1},{1,2},{2,3},{3,0},{4,5},{5,6},{6,7},{7,4},{8,9},{9,10},{10,1... | collective-permute-start | bytes 1966088 | tf_op jit(solution)/shard_map/ppermute | solution.py:131
  96.7 10.5 %all-to-all-start.1 = ((f32[16,1,768]{2,1,0:T(1,128)}), f32[16,1,768]{2,1,0:T(1,128)S(1)}, u32[]{:S(2)}, u32[]{:S(2)}) async-start(f32[16,1,768]{2,1,0:T(1,128)} %broadcast_in_dim.111), calls=%async_computation.1 | async-start | bytes 98304 | tf_op jit(solution)/shard_map/all_to_all | solution.py:40
  100.8 33.3 %collective-permute-start.8 = (bf16[5120,256]{1,0:T(8,128)(2,1)S(1)}, bf16[5120,256]{1,0:T(8,128)(2,1)}, u32[]{:S(2)}, u32[]{:S(2)}) collective-permute-start(bf16[5120,256]{1,0:T(8,128)(2,1)S(1)} %bitcast.43), channel_id=1, source_target_pairs={{0,16},{16,0},{1,17},{17,1},{2,18},{18,2},{3,19},{19,3},{4,20},{20... | collective-permute-start | bytes 7864328 | tf_op jit(solution)/shard_map/ppermute | solution.py:144
  108.0 18.1 %all-to-all-start.2 = ((f32[16,1,768]{2,1,0:T(1,128)}), f32[16,1,768]{2,1,0:T(1,128)S(1)}, u32[]{:S(2)}, u32[]{:S(2)}) async-start(f32[16,1,768]{2,1,0:T(1,128)} %broadcast_in_dim.113), calls=%async_computation.2 | async-start | bytes 98304 | tf_op jit(solution)/shard_map/all_to_all | solution.py:40

commit v4 on v3

--- a/solution.py
+++ b/solution.py
@@ -132,19 +132,20 @@
 
     student_b, teacher_a = pass_on(student_1, 1), pass_on(teacher_1, 3)
     student_a, teacher_b = pass_on(student_1, 3), pass_on(teacher_1, 1)
-    student_b, teacher_a, student_other, teacher_other = lax.optimization_barrier(
-        (student_b, teacher_a, student_other, teacher_other)
-    )
+    student_b, student_other = lax.optimization_barrier((student_b, student_other))
+    teacher_a, teacher_other = lax.optimization_barrier((teacher_a, teacher_other))
     student_c, teacher_c = pass_on(student_b, 1), pass_on(teacher_a, 3)
     near_s = place((student_1, student_b, student_a), (0, 1, 3))
     near_t = place((teacher_1, teacher_b, teacher_a), (0, 1, 3))
+    head_s = jnp.concatenate([student_head, student_other], axis=0)
+    head_t = jnp.concatenate([teacher_head, teacher_other], axis=0)
+    near_s, head_s = lax.optimization_barrier((near_s, head_s))
+    near_t, head_t = lax.optimization_barrier((near_t, head_t))
     student_t = place((student_c,), (2,), (near_s,)).reshape(width, cols)
     teacher_t = place((teacher_c,), (2,), (near_t,)).reshape(width, cols)
 
     student_mate = lax.ppermute(student_t, "core", SWAP)
 
-    head_s = jnp.concatenate([student_head, student_other], axis=0)
-    head_t = jnp.concatenate([teacher_head, teacher_other], axis=0)
     ls = jnp.dot(head_s, student_t, preferred_element_type=f32)
     lt = jnp.dot(head_t, teacher_t, preferred_element_type=f32)
     source, block_weight = block_sources(route, groups, TASKS, BLK, groups * per_group)

time: 140 us -> 137 us (0.979)
  matrix products: 11.3 us -> 7.55 us
  other arithmetic: 1.82 us -> 5.03 us
  Pallas kernels: 2.59 us -> 0.41 us
    concatenate x0 -> x2, other arithmetic: none -> 3.21 us  [the longest x1 1.6 us: per_device(): head_t = jnp.concatenate([teacher_head, teacher_other], axis=0)]
    pallas_call x4, Pallas kernels: 2.59 us -> 0.41 us  [place(): pl.pallas_call(functools.partial(place_kernel, shifts), out_shape=jax.Sha...]
    dot_general x1, matrix products: 2.89 us -> 0.98 us  [per_device(): lt = jnp.dot(head_t, teacher_t, preferred_element_type=f32)]
    dot_general x1, matrix products: 2.85 us -> 1 us  [per_device(): ls = jnp.dot(head_s, student_t, preferred_element_type=f32)]
  transfers between devices with their start and end apart: 12 -> 12, of which waited for: 6 -> 6; matrix products, arithmetic and copies ran while one was open for 4% -> 5% of each run, Pallas kernels for 2% -> 0%
where the time goes in v4:
time: 137 us; the launch traced here: 136 us
  blocking collectives  48 us (35%)
  starting transfers between devices  42.6 us (31%)
  waiting for transfers between devices  26.5 us (19%)
  matrix products  7.55 us (6%)
  other arithmetic  5.03 us (4%)
  local copies, waits for them, and re-layouts  4.71 us (3%)
    all_gather x1, blocking collectives, per_device(): got = lax.all_gather(held, ('z', 'core'))  40.2 us
    ppermute x6, starting transfers between devices, pass_on(): lax.ppermute(piece, plane, [(i[j], i[(j + k) % len(i)]) for i in LAST for...  18.6 us
    all_to_all x2, waiting for transfers between devices, spread(): return lax.all_to_all(jnp.broadcast_to(x[None], (n,) + x.shape), axes, 0, 0)  11.8 us
    all_to_all x2, starting transfers between devices, spread(): return lax.all_to_all(jnp.broadcast_to(x[None], (n,) + x.shape), axes, 0, 0)  9.94 us
    ppermute x6, waiting for transfers between devices, pass_on(): lax.ppermute(piece, plane, [(i[j], i[(j + k) % len(i)]) for i in LAST for...  7.93 us
    all_gather x1, blocking collectives, per_device(): grad_in = lax.all_gather(grad[rows:], 'core')  7.82 us
    all_to_all x1, waiting for transfers between devices, spread_groups(): return lax.all_to_all(copies, axes, 0, 0, axis_index_groups=lines)  6.78 us
    ppermute x1, starting transfers between devices, per_device(): student_mate = lax.ppermute(student_t, 'core', SWAP)  5.57 us
  transfers between devices with their start and end apart: 12, of which 6 were waited for; matrix products, arithmetic and copies ran while one was open for 5% of the time, Pallas kernels for 0%

profile of v4, /device:TPU:1, one launch (start us, length us, event | category | flops | bytes accessed | tf_op | source)
XLA Modules:
  0.0 136.0 jit_solution(8094234947439228498)
XLA Ops:
  2.3 40.2 %all-gather = bf16[1280,320]{1,0:T(8,128)(2,1)S(1)} all-gather(bf16[40,320]{1,0:T(8,128)(2,1)S(1)} %pad_maximum_fusion.3), channel_id=2, replica_groups=mesh['z'=16,'core'=2,'x'=4,'y'=4] {'z','core'}, dimensions={0}, use_global_device_ids=true | all-gather | bytes 844800 | tf_op jit(solution)/shard_map/all_gather | solution.py:108
  43.5 1.1 broadcast_in_dim.110
  44.7 4.2 %all-to-all-start = ((bf16[4,2,320,256]{3,2,1,0:T(8,128)(2,1)}), bf16[4,2,320,256]{3,2,1,0:T(8,128)(2,1)S(1)}, u32[]{:S(2)}, u32[]{:S(2)}) async-start(bf16[4,2,320,256]{3,2,1,0:T(8,128)(2,1)} %broadcast_in_dim.110), calls=%async_computation | async-start | bytes 2621440 | tf_op jit(solution)/shard_map/all_to_all | solution.py:64
  48.9 2.2 %collective-permute-start.6 = (bf16[152,5120]{1,0:T(8,128)(2,1)S(1)}, bf16[152,5120]{1,0:T(8,128)(2,1)}, u32[]{:S(2)}, u32[]{:S(2)}) collective-permute-start(bf16[152,5120]{1,0:T(8,128)(2,1)S(1)} %copy-done), channel_id=1, source_target_pairs={{0,16},{16,0},{1,17},{17,1},{2,18},{18,2},{3,19},{19,3},{4,20},{20... | collective-permute-start | bytes 4669448 | tf_op jit(solution)/shard_map/ppermute | solution.py:123
  51.0 2.2 %collective-permute-start.1 = (bf16[152,5120]{1,0:T(8,128)(2,1)}, bf16[152,5120]{1,0:T(8,128)(2,1)}, u32[]{:S(2)}, u32[]{:S(2)}) collective-permute-start(bf16[152,5120]{1,0:T(8,128)(2,1)} %param.7), channel_id=1, source_target_pairs={{0,16},{16,0},{1,17},{17,1},{2,18},{18,2},{3,19},{19,3},{4,20},{20... | collective-permute-start | bytes 4669448 | tf_op jit(solution)/shard_map/ppermute | solution.py:122
  53.5 6.8 %all-to-all-done = bf16[4,2,320,256]{3,2,1,0:T(8,128)(2,1)S(1)} async-done(((bf16[4,2,320,256]{3,2,1,0:T(8,128)(2,1)}), bf16[4,2,320,256]{3,2,1,0:T(8,128)(2,1)S(1)}, u32[]{:S(2)}, u32[]{:S(2)}) %all-to-all-start) | async-done | bytes 1310752 | tf_op jit(solution)/shard_map/all_to_all | solution.py:64
  60.4 4.1 %collective-permute-start.5 = (bf16[4,320,256]{2,1,0:T(8,128)(2,1)S(1)}, bf16[4,320,256]{2,1,0:T(8,128)(2,1)S(1)}, u32[]{:S(2)}, u32[]{:S(2)}) collective-permute-start(bf16[4,320,256]{2,1,0:T(8,128)(2,1)S(1)} %get-tuple-element.25.refs_0_), channel_id=1, source_target_pairs={{0,3},{1,0},{2,1},{3,2},{4,7},{5,4},{6,5},{7,6},{8,11},{9,8},{10,9... | collective-permute-start | bytes 1966088 | tf_op jit(solution)/shard_map/ppermute | solution.py:131
  64.5 1.9 %collective-permute-start = (bf16[4,320,256]{2,1,0:T(8,128)(2,1)S(1)}, bf16[4,320,256]{2,1,0:T(8,128)(2,1)S(1)}, u32[]{:S(2)}, u32[]{:S(2)}) collective-permute-start(bf16[4,320,256]{2,1,0:T(8,128)(2,1)S(1)} %get-tuple-element.26.refs_0_), channel_id=1, source_target_pairs={{0,1},{1,2},{2,3},{3,0},{4,5},{5,6},{6,7},{7,4},{8,9},{9,10},{10,1... | collective-permute-start | bytes 1966088 | tf_op jit(solution)/shard_map/ppermute | solution.py:131
  66.6 2.2 %collective-permute-start.4 = (bf16[4,320,256]{2,1,0:T(8,128)(2,1)S(1)}, bf16[4,320,256]{2,1,0:T(8,128)(2,1)S(1)}, u32[]{:S(2)}, u32[]{:S(2)}) collective-permute-start(bf16[4,320,256]{2,1,0:T(8,128)(2,1)S(1)} %get-tuple-element.25.refs_0_), channel_id=1, source_target_pairs={{0,1},{1,2},{2,3},{3,0},{4,5},{5,6},{6,7},{7,4},{8,9},{9,10},{10,1... | collective-permute-start | bytes 1966088 | tf_op jit(solution)/shard_map/ppermute | solution.py:131
  68.8 4.4 %collective-permute-start.2 = (bf16[4,320,256]{2,1,0:T(8,128)(2,1)S(1)}, bf16[4,320,256]{2,1,0:T(8,128)(2,1)S(1)}, u32[]{:S(2)}, u32[]{:S(2)}) collective-permute-start(bf16[4,320,256]{2,1,0:T(8,128)(2,1)S(1)} %get-tuple-element.26.refs_0_), channel_id=1, source_target_pairs={{0,3},{1,0},{2,1},{3,2},{4,7},{5,4},{6,5},{7,6},{8,11},{9,8},{10,9... | collective-permute-start | bytes 1966088 | tf_op jit(solution)/shard_map/ppermute | solution.py:131
  73.3 4.0 %collective-permute-start.7 = (bf16[4,320,256]{2,1,0:T(8,128)(2,1)S(1)}, bf16[4,320,256]{2,1,0:T(8,128)(2,1)S(1)}, u32[]{:S(2)}, u32[]{:S(2)}) collective-permute-start(bf16[4,320,256]{2,1,0:T(8,128)(2,1)S(1)} %collective-permute-done.5.refs_2_), channel_id=1, source_target_pairs={{0,3},{1,0},{2,1},{3,2},{4,7},{5,4},{6,5},{7,6},{8,11},{9,8},{10,9... | collective-permute-start | bytes 1966088 | tf_op jit(solution)/shard_map/ppermute | solution.py:131
  77.3 1.6 %pad_maximum_fusion.1 = bf16[304,5120]{1,0:T(8,128)(2,1)S(1)} fusion(bf16[152,5120]{1,0:T(8,128)(2,1)} %collective-permute-done.6, bf16[152,5120]{1,0:T(8,128)(2,1)S(1)} %copy-done), kind=kLoop, calls=%fused_computation.5 | loop fusion | flops 6225920 | bytes 6225920 | tf_op jit(solution)/shard_map/concatenate | solution.py:141
  78.9 1.9 %collective-permute-start.3 = (bf16[4,320,256]{2,1,0:T(8,128)(2,1)S(1)}, bf16[4,320,256]{2,1,0:T(8,128)(2,1)S(1)}, u32[]{:S(2)}, u32[]{:S(2)}) collective-permute-start(bf16[4,320,256]{2,1,0:T(8,128)(2,1)S(1)} %collective-permute-done.refs_1_), channel_id=1, source_target_pairs={{0,1},{1,2},{2,3},{3,0},{4,5},{5,6},{6,7},{7,4},{8,9},{9,10},{10,1... | collective-permute-start | bytes 1966088 | tf_op jit(solution)/shard_map/ppermute | solution.py:131
  80.9 1.6 %pad_maximum_fusion = bf16[304,5120]{1,0:T(8,128)(2,1)S(1)} fusion(bf16[152,5120]{1,0:T(8,128)(2,1)} %collective-permute-done.1, bf16[152,5120]{1,0:T(8,128)(2,1)S(1)} %copy-done.1), kind=kLoop, calls=%fused_computation.4 | loop fusion | flops 6225920 | bytes 6225920 | tf_op jit(solution)/shard_map/concatenate | solution.py:140
  82.5 1.9 %collective-permute-done.4.refs_1_ = bf16[4,320,256]{2,1,0:T(8,128)(2,1)S(1)} collective-permute-done((bf16[4,320,256]{2,1,0:T(8,128)(2,1)S(1)}, bf16[4,320,256]{2,1,0:T(8,128)(2,1)S(1)}, u32[]{:S(2)}, u32[]{:S(2)}) %collective-permute-start.4) | collective-permute-done | bytes 655392 | tf_op jit(solution)/shard_map/ppermute | solution.py:131
  84.7 3.1 %collective-permute-done.7.refs_0_ = bf16[4,320,256]{2,1,0:T(8,128)(2,1)S(1)} collective-permute-done((bf16[4,320,256]{2,1,0:T(8,128)(2,1)S(1)}, bf16[4,320,256]{2,1,0:T(8,128)(2,1)S(1)}, u32[]{:S(2)}, u32[]{:S(2)}) %collective-permute-start.7) | collective-permute-done | bytes 655392 | tf_op jit(solution)/shard_map/ppermute | solution.py:131
  88.8 2.9 %collective-permute-done.3.refs_0_ = bf16[4,320,256]{2,1,0:T(8,128)(2,1)S(1)} collective-permute-done((bf16[4,320,256]{2,1,0:T(8,128)(2,1)S(1)}, bf16[4,320,256]{2,1,0:T(8,128)(2,1)S(1)}, u32[]{:S(2)}, u32[]{:S(2)}) %collective-permute-start.3) | collective-permute-done | bytes 655392 | tf_op jit(solution)/shard_map/ppermute | solution.py:131
  91.8 1.0 fusion.30
  93.7 3.5 %all-to-all-start.1 = ((f32[16,1,768]{2,1,0:T(1,128)}), f32[16,1,768]{2,1,0:T(1,128)S(1)}, u32[]{:S(2)}, u32[]{:S(2)}) async-start(f32[16,1,768]{2,1,0:T(1,128)} %broadcast_in_dim.111), calls=%async_computation.1 | async-start | bytes 98304 | tf_op jit(solution)/shard_map/all_to_all | solution.py:40
  97.3 5.6 %collective-permute-start.8 = (bf16[5120,256]{1,0:T(8,128)(2,1)S(1)}, bf16[5120,256]{1,0:T(8,128)(2,1)}, u32[]{:S(2)}, u32[]{:S(2)}) collective-permute-start(bf16[5120,256]{1,0:T(8,128)(2,1)S(1)} %bitcast.45), channel_id=1, source_target_pairs={{0,16},{16,0},{1,17},{17,1},{2,18},{18,2},{3,19},{19,3},{4,20},{20... | collective-permute-start | bytes 7864328 | tf_op jit(solution)/shard_map/ppermute | solution.py:147
  104.4 6.4 %all-to-all-start.2 = ((f32[16,1,768]{2,1,0:T(1,128)}), f32[16,1,768]{2,1,0:T(1,128)S(1)}, u32[]{:S(2)}, u32[]{:S(2)}) async-start(f32[16,1,768]{2,1,0:T(1,128)} %broadcast_in_dim.113), calls=%async_computation.2 | async-start | bytes 98304 | tf_op jit(solution)/shard_map/all_to_all | solution.py:40
  111.4 11.1 %all-to-all-done.2 = f32[16,1,768]{2,1,0:T(1,128)S(1)} async-done(((f32[16,1,768]{2,1,0:T(1,128)}), f32[16,1,768]{2,1,0:T(1,128)S(1)}, u32[]{:S(2)}, u32[]{:S(2)}) %all-to-all-start.2) | async-done | bytes 49184 | tf_op jit(solution)/shard_map/all_to_all | solution.py:40
  123.4 7.8 %all-gather.1 = bf16[304,256]{1,0:T(8,128)(2,1)S(1)} all-gather(bf16[152,256]{1,0:T(8,128)(2,1)S(1)} %get-tuple-element.30), channel_id=3, replica_groups=mesh['z'=16,'core'=2,'x'=4,'y'=4] {'core'}, dimensions={0}, use_global_device_ids=true | all-gather | bytes 233472 | tf_op jit(solution)/shard_map/all_gather | solution.py:168
  131.3 4.7 %convolution_convert_fusion = bf16[152,5120]{1,0:T(8,128)(2,1)} fusion(bf16[5120,256]{1,0:T(8,128)(2,1)} %collective-permute-done.8, bf16[5120,256]{1,0:T(8,128)(2,1)S(1)} %bitcast.46, bf16[152,256]{1,0:T(8,128)(2,1)S(1)} %dynamic-slice_bitcast_fusion, bf16[152,256]{1,0:T(8,128)(2,1)S(1)} %get-tuple-element.29), kind=kOutput, calls=%fused_computation | convolution fusion | flops 808493056 | bytes 6955008 | tf_op jit(solution)/shard_map/dot_general | solution.py:171
  (74 shorter events, 8.4 us)
Async XLA Ops:
  43.4 5.4 %copy-start = (bf16[152,5120]{1,0:T(8,128)(2,1)S(1)}, bf16[152,5120]{1,0:T(8,128)(2,1)}, u32[]{:S(2)}) copy-start(bf16[152,5120]{1,0:T(8,128)(2,1)} %param.8) | copy-start | bytes 4669444
  43.5 9.7 %copy-start.2 = (s32[32,3]{0,1:T(4,128)S(1)}, s32[32,3]{0,1:T(4,128)}, u32[]{:S(2)}) copy-start(s32[32,3]{0,1:T(4,128)} %param.9) | copy-start | bytes 1156
  44.7 15.6 %all-to-all-start = ((bf16[4,2,320,256]{3,2,1,0:T(8,128)(2,1)}), bf16[4,2,320,256]{3,2,1,0:T(8,128)(2,1)S(1)}, u32[]{:S(2)}, u32[]{:S(2)}) async-start(bf16[4,2,320,256]{3,2,1,0:T(8,128)(2,1)} %broadcast_in_dim.110), calls=%async_computation | async-start | bytes 2621440 | tf_op jit(solution)/shard_map/all_to_all | solution.py:64
  48.9 20.0 %collective-permute-start.6 = (bf16[152,5120]{1,0:T(8,128)(2,1)S(1)}, bf16[152,5120]{1,0:T(8,128)(2,1)}, u32[]{:S(2)}, u32[]{:S(2)}) collective-permute-start(bf16[152,5120]{1,0:T(8,128)(2,1)S(1)} %copy-done), channel_id=1, source_target_pairs={{0,16},{16,0},{1,17},{17,1},{2,18},{18,2},{3,19},{19,3},{4,20},{20... | collective-permute-start | bytes 4669448 | tf_op jit(solution)/shard_map/ppermute | solution.py:123
  51.0 27.9 %collective-permute-start.1 = (bf16[152,5120]{1,0:T(8,128)(2,1)}, bf16[152,5120]{1,0:T(8,128)(2,1)}, u32[]{:S(2)}, u32[]{:S(2)}) collective-permute-start(bf16[152,5120]{1,0:T(8,128)(2,1)} %param.7), channel_id=1, source_target_pairs={{0,16},{16,0},{1,17},{17,1},{2,18},{18,2},{3,19},{19,3},{4,20},{20... | collective-permute-start | bytes 4669448 | tf_op jit(solution)/shard_map/ppermute | solution.py:122
  60.4 12.9 %collective-permute-start.5 = (bf16[4,320,256]{2,1,0:T(8,128)(2,1)S(1)}, bf16[4,320,256]{2,1,0:T(8,128)(2,1)S(1)}, u32[]{:S(2)}, u32[]{:S(2)}) collective-permute-start(bf16[4,320,256]{2,1,0:T(8,128)(2,1)S(1)} %get-tuple-element.25.refs_0_), channel_id=1, source_target_pairs={{0,3},{1,0},{2,1},{3,2},{4,7},{5,4},{6,5},{7,6},{8,11},{9,8},{10,9... | collective-permute-start | bytes 1966088 | tf_op jit(solution)/shard_map/ppermute | solution.py:131
  64.5 14.4 %collective-permute-start = (bf16[4,320,256]{2,1,0:T(8,128)(2,1)S(1)}, bf16[4,320,256]{2,1,0:T(8,128)(2,1)S(1)}, u32[]{:S(2)}, u32[]{:S(2)}) collective-permute-start(bf16[4,320,256]{2,1,0:T(8,128)(2,1)S(1)} %get-tuple-element.26.refs_0_), channel_id=1, source_target_pairs={{0,1},{1,2},{2,3},{3,0},{4,5},{5,6},{6,7},{7,4},{8,9},{9,10},{10,1... | collective-permute-start | bytes 1966088 | tf_op jit(solution)/shard_map/ppermute | solution.py:131
  66.6 14.3 %copy-start.1 = (bf16[152,5120]{1,0:T(8,128)(2,1)S(1)}, bf16[152,5120]{1,0:T(8,128)(2,1)}, u32[]{:S(2)}) copy-start(bf16[152,5120]{1,0:T(8,128)(2,1)} %param.7) | copy-start | bytes 4669444
  66.6 17.8 %collective-permute-start.4 = (bf16[4,320,256]{2,1,0:T(8,128)(2,1)S(1)}, bf16[4,320,256]{2,1,0:T(8,128)(2,1)S(1)}, u32[]{:S(2)}, u32[]{:S(2)}) collective-permute-start(bf16[4,320,256]{2,1,0:T(8,128)(2,1)S(1)} %get-tuple-element.25.refs_0_), channel_id=1, source_target_pairs={{0,1},{1,2},{2,3},{3,0},{4,5},{5,6},{6,7},{7,4},{8,9},{9,10},{10,1... | collective-permute-start | bytes 1966088 | tf_op jit(solution)/shard_map/ppermute | solution.py:131
  68.8 15.7 %collective-permute-start.2 = (bf16[4,320,256]{2,1,0:T(8,128)(2,1)S(1)}, bf16[4,320,256]{2,1,0:T(8,128)(2,1)S(1)}, u32[]{:S(2)}, u32[]{:S(2)}) collective-permute-start(bf16[4,320,256]{2,1,0:T(8,128)(2,1)S(1)} %get-tuple-element.26.refs_0_), channel_id=1, source_target_pairs={{0,3},{1,0},{2,1},{3,2},{4,7},{5,4},{6,5},{7,6},{8,11},{9,8},{10,9... | collective-permute-start | bytes 1966088 | tf_op jit(solution)/shard_map/ppermute | solution.py:131
  73.3 14.5 %collective-permute-start.7 = (bf16[4,320,256]{2,1,0:T(8,128)(2,1)S(1)}, bf16[4,320,256]{2,1,0:T(8,128)(2,1)S(1)}, u32[]{:S(2)}, u32[]{:S(2)}) collective-permute-start(bf16[4,320,256]{2,1,0:T(8,128)(2,1)S(1)} %collective-permute-done.5.refs_2_), channel_id=1, source_target_pairs={{0,3},{1,0},{2,1},{3,2},{4,7},{5,4},{6,5},{7,6},{8,11},{9,8},{10,9... | collective-permute-start | bytes 1966088 | tf_op jit(solution)/shard_map/ppermute | solution.py:131
  78.9 12.8 %collective-permute-start.3 = (bf16[4,320,256]{2,1,0:T(8,128)(2,1)S(1)}, bf16[4,320,256]{2,1,0:T(8,128)(2,1)S(1)}, u32[]{:S(2)}, u32[]{:S(2)}) collective-permute-start(bf16[4,320,256]{2,1,0:T(8,128)(2,1)S(1)} %collective-permute-done.refs_1_), channel_id=1, source_target_pairs={{0,1},{1,2},{2,3},{3,0},{4,5},{5,6},{6,7},{7,4},{8,9},{9,10},{10,1... | collective-permute-start | bytes 1966088 | tf_op jit(solution)/shard_map/ppermute | solution.py:131
  93.7 9.9 %all-to-all-start.1 = ((f32[16,1,768]{2,1,0:T(1,128)}), f32[16,1,768]{2,1,0:T(1,128)S(1)}, u32[]{:S(2)}, u32[]{:S(2)}) async-start(f32[16,1,768]{2,1,0:T(1,128)} %broadcast_in_dim.111), calls=%async_computation.1 | async-start | bytes 98304 | tf_op jit(solution)/shard_map/all_to_all | solution.py:40
  97.3 34.0 %collective-permute-start.8 = (bf16[5120,256]{1,0:T(8,128)(2,1)S(1)}, bf16[5120,256]{1,0:T(8,128)(2,1)}, u32[]{:S(2)}, u32[]{:S(2)}) collective-permute-start(bf16[5120,256]{1,0:T(8,128)(2,1)S(1)} %bitcast.45), channel_id=1, source_target_pairs={{0,16},{16,0},{1,17},{17,1},{2,18},{18,2},{3,19},{19,3},{4,20},{20... | collective-permute-start | bytes 7864328 | tf_op jit(solution)/shard_map/ppermute | solution.py:147
  104.4 18.0 %all-to-all-start.2 = ((f32[16,1,768]{2,1,0:T(1,128)}), f32[16,1,768]{2,1,0:T(1,128)S(1)}, u32[]{:S(2)}, u32[]{:S(2)}) async-start(f32[16,1,768]{2,1,0:T(1,128)} %broadcast_in_dim.113), calls=%async_computation.2 | async-start | bytes 98304 | tf_op jit(solution)/shard_map/all_to_all | solution.py:40

commit v5 on v4

--- a/solution.py
+++ b/solution.py
@@ -86,7 +86,7 @@
         in_specs=[whole] * (n + len(into)),
         out_specs=whole,
         input_output_aliases={n: 0} if into else {},
-        compiler_params=pltpu.CompilerParams(vmem_limit_bytes=8 * 1024 * 1024),
+        compiler_params=pltpu.CompilerParams(vmem_limit_bytes=4 * 1024 * 1024),
         name="place_blocks",
     )(*pieces, *(pltpu.with_memory_space_constraint(b, pltpu.VMEM) for b in into))
 
@@ -168,12 +168,10 @@
     grad_in = lax.all_gather(grad[rows:], "core")
     grad_in = lax.dynamic_index_in_dim(grad_in, 1 - core, 0, keepdims=False)
     nt = (((1,), (1,)), ((), ()))
-    head_grad = lax.dot_general(
-        jnp.concatenate([grad[:rows], grad_in], axis=1),
-        jnp.concatenate([student_t, student_mate], axis=1),
-        nt,
-        preferred_element_type=f32,
-    ).astype(bf16)
+    student_mate = lax.optimization_barrier(jnp.where(z >= 0, student_mate, -student_mate))
+    head_grad = lax.dot_general(grad_in, student_mate, nt, preferred_element_type=f32)
+    head_grad += lax.dot_general(grad[:rows], student_t, nt, preferred_element_type=f32)
+    head_grad = head_grad.astype(bf16)
     own = lax.dynamic_index_in_dim(stats.reshape(6, NZ, BLK), z, 1, keepdims=False)
     own = own.reshape(3, per_group)
     loss = own[2] - own[0] + own[1]

time: 137 us -> 136 us (level)
  other arithmetic: 5.03 us -> 6.96 us
  matrix products: 7.55 us -> 5.99 us
    select_n x0 -> x1, other arithmetic: none -> 1.93 us  [per_device(): jnp.where(z >= 0, student_mate, -student_mate)]
    dot_general x1 -> x2, matrix products: 4.74 us -> 3.18 us  [the longest x1 2.17 us: per_device(): lax.dot_general(grad_in, student_mate, nt, preferred_element_type=f32)]
  transfers between devices with their start and end apart: 12 -> 12, of which waited for: 6 -> 5; matrix products, arithmetic and copies ran while one was open for 5% -> 6% of each run, Pallas kernels for 0% -> 0%
where the time goes in v5:
time: 136 us; the launch traced here: 135 us
  blocking collectives  47.7 us (35%)
  starting transfers between devices  42.1 us (31%)
  waiting for transfers between devices  26.3 us (19%)
  other arithmetic  6.96 us (5%)
  matrix products  5.99 us (4%)
  local copies, waits for them, and re-layouts  4.7 us (3%)
    all_gather x1, blocking collectives, per_device(): got = lax.all_gather(held, ('z', 'core'))  40.2 us
    ppermute x6, starting transfers between devices, pass_on(): lax.ppermute(piece, plane, [(i[j], i[(j + k) % len(i)]) for i in LAST for...  18.4 us
    all_to_all x2, waiting for transfers between devices, spread(): return lax.all_to_all(jnp.broadcast_to(x[None], (n,) + x.shape), axes, 0, 0)  12.1 us
    all_to_all x2, starting transfers between devices, spread(): return lax.all_to_all(jnp.broadcast_to(x[None], (n,) + x.shape), axes, 0, 0)  9.94 us
    all_gather x1, blocking collectives, per_device(): grad_in = lax.all_gather(grad[rows:], 'core')  7.52 us
    ppermute x6, waiting for transfers between devices, pass_on(): lax.ppermute(piece, plane, [(i[j], i[(j + k) % len(i)]) for i in LAST for...  7.37 us
    all_to_all x1, waiting for transfers between devices, spread_groups(): return lax.all_to_all(copies, axes, 0, 0, axis_index_groups=lines)  6.78 us
    ppermute x1, starting transfers between devices, per_device(): student_mate = lax.ppermute(student_t, 'core', SWAP)  5.27 us
  transfers between devices with their start and end apart: 12, of which 5 were waited for; matrix products, arithmetic and copies ran while one was open for 6% of the time, Pallas kernels for 0%

profile of v5, /device:TPU:1, one launch (start us, length us, event | category | flops | bytes accessed | tf_op | source)
XLA Modules:
  0.0 135.3 jit_solution(1809570324610737297)
XLA Ops:
  2.3 40.2 %all-gather = bf16[1280,320]{1,0:T(8,128)(2,1)S(1)} all-gather(bf16[40,320]{1,0:T(8,128)(2,1)S(1)} %pad_maximum_fusion.3), channel_id=2, replica_groups=mesh['z'=16,'core'=2,'x'=4,'y'=4] {'z','core'}, dimensions={0}, use_global_device_ids=true | all-gather | bytes 844800 | tf_op jit(solution)/shard_map/all_gather | solution.py:108
  43.5 1.1 broadcast_in_dim.110
  44.7 4.2 %all-to-all-start = ((bf16[4,2,320,256]{3,2,1,0:T(8,128)(2,1)}), bf16[4,2,320,256]{3,2,1,0:T(8,128)(2,1)S(1)}, u32[]{:S(2)}, u32[]{:S(2)}) async-start(bf16[4,2,320,256]{3,2,1,0:T(8,128)(2,1)} %broadcast_in_dim.110), calls=%async_computation | async-start | bytes 2621440 | tf_op jit(solution)/shard_map/all_to_all | solution.py:64
  48.9 2.2 %collective-permute-start.1 = (bf16[152,5120]{1,0:T(8,128)(2,1)S(1)}, bf16[152,5120]{1,0:T(8,128)(2,1)}, u32[]{:S(2)}, u32[]{:S(2)}) collective-permute-start(bf16[152,5120]{1,0:T(8,128)(2,1)S(1)} %copy-done), channel_id=1, source_target_pairs={{0,16},{16,0},{1,17},{17,1},{2,18},{18,2},{3,19},{19,3},{4,20},{20... | collective-permute-start | bytes 4669448 | tf_op jit(solution)/shard_map/ppermute | solution.py:122
  51.0 2.2 %collective-permute-start.6 = (bf16[152,5120]{1,0:T(8,128)(2,1)}, bf16[152,5120]{1,0:T(8,128)(2,1)}, u32[]{:S(2)}, u32[]{:S(2)}) collective-permute-start(bf16[152,5120]{1,0:T(8,128)(2,1)} %param.8), channel_id=1, source_target_pairs={{0,16},{16,0},{1,17},{17,1},{2,18},{18,2},{3,19},{19,3},{4,20},{20... | collective-permute-start | bytes 4669448 | tf_op jit(solution)/shard_map/ppermute | solution.py:123
  53.5 6.8 %all-to-all-done = bf16[4,2,320,256]{3,2,1,0:T(8,128)(2,1)S(1)} async-done(((bf16[4,2,320,256]{3,2,1,0:T(8,128)(2,1)}), bf16[4,2,320,256]{3,2,1,0:T(8,128)(2,1)S(1)}, u32[]{:S(2)}, u32[]{:S(2)}) %all-to-all-start) | async-done | bytes 1310752 | tf_op jit(solution)/shard_map/all_to_all | solution.py:64
  60.4 2.8 %collective-permute-start = (bf16[4,320,256]{2,1,0:T(8,128)(2,1)S(1)}, bf16[4,320,256]{2,1,0:T(8,128)(2,1)S(1)}, u32[]{:S(2)}, u32[]{:S(2)}) collective-permute-start(bf16[4,320,256]{2,1,0:T(8,128)(2,1)S(1)} %get-tuple-element.26.refs_0_), channel_id=1, source_target_pairs={{0,1},{1,2},{2,3},{3,0},{4,5},{5,6},{6,7},{7,4},{8,9},{9,10},{10,1... | collective-permute-start | bytes 1966088 | tf_op jit(solution)/shard_map/ppermute | solution.py:131
  63.3 3.7 %collective-permute-start.5 = (bf16[4,320,256]{2,1,0:T(8,128)(2,1)S(1)}, bf16[4,320,256]{2,1,0:T(8,128)(2,1)S(1)}, u32[]{:S(2)}, u32[]{:S(2)}) collective-permute-start(bf16[4,320,256]{2,1,0:T(8,128)(2,1)S(1)} %get-tuple-element.25.refs_0_), channel_id=1, source_target_pairs={{0,3},{1,0},{2,1},{3,2},{4,7},{5,4},{6,5},{7,6},{8,11},{9,8},{10,9... | collective-permute-start | bytes 1966088 | tf_op jit(solution)/shard_map/ppermute | solution.py:131
  67.1 3.0 %collective-permute-start.2 = (bf16[4,320,256]{2,1,0:T(8,128)(2,1)S(1)}, bf16[4,320,256]{2,1,0:T(8,128)(2,1)S(1)}, u32[]{:S(2)}, u32[]{:S(2)}) collective-permute-start(bf16[4,320,256]{2,1,0:T(8,128)(2,1)S(1)} %get-tuple-element.26.refs_0_), channel_id=1, source_target_pairs={{0,3},{1,0},{2,1},{3,2},{4,7},{5,4},{6,5},{7,6},{8,11},{9,8},{10,9... | collective-permute-start | bytes 1966088 | tf_op jit(solution)/shard_map/ppermute | solution.py:131
  70.1 2.4 %collective-permute-start.4 = (bf16[4,320,256]{2,1,0:T(8,128)(2,1)S(1)}, bf16[4,320,256]{2,1,0:T(8,128)(2,1)S(1)}, u32[]{:S(2)}, u32[]{:S(2)}) collective-permute-start(bf16[4,320,256]{2,1,0:T(8,128)(2,1)S(1)} %get-tuple-element.25.refs_0_), channel_id=1, source_target_pairs={{0,1},{1,2},{2,3},{3,0},{4,5},{5,6},{6,7},{7,4},{8,9},{9,10},{10,1... | collective-permute-start | bytes 1966088 | tf_op jit(solution)/shard_map/ppermute | solution.py:131
  73.2 1.9 %collective-permute-start.3 = (bf16[4,320,256]{2,1,0:T(8,128)(2,1)S(1)}, bf16[4,320,256]{2,1,0:T(8,128)(2,1)S(1)}, u32[]{:S(2)}, u32[]{:S(2)}) collective-permute-start(bf16[4,320,256]{2,1,0:T(8,128)(2,1)S(1)} %collective-permute-done.refs_1_), channel_id=1, source_target_pairs={{0,1},{1,2},{2,3},{3,0},{4,5},{5,6},{6,7},{7,4},{8,9},{9,10},{10,1... | collective-permute-start | bytes 1966088 | tf_op jit(solution)/shard_map/ppermute | solution.py:131
  75.1 1.6 %pad_maximum_fusion = bf16[304,5120]{1,0:T(8,128)(2,1)S(1)} fusion(bf16[152,5120]{1,0:T(8,128)(2,1)} %collective-permute-done.1, bf16[152,5120]{1,0:T(8,128)(2,1)S(1)} %copy-done), kind=kLoop, calls=%fused_computation.3 | loop fusion | flops 6225920 | bytes 6225920 | tf_op jit(solution)/shard_map/concatenate | solution.py:140
  76.8 4.6 %collective-permute-start.7 = (bf16[4,320,256]{2,1,0:T(8,128)(2,1)S(1)}, bf16[4,320,256]{2,1,0:T(8,128)(2,1)S(1)}, u32[]{:S(2)}, u32[]{:S(2)}) collective-permute-start(bf16[4,320,256]{2,1,0:T(8,128)(2,1)S(1)} %collective-permute-done.5.refs_2_), channel_id=1, source_target_pairs={{0,3},{1,0},{2,1},{3,2},{4,7},{5,4},{6,5},{7,6},{8,11},{9,8},{10,9... | collective-permute-start | bytes 1966088 | tf_op jit(solution)/shard_map/ppermute | solution.py:131
  81.4 1.6 %pad_maximum_fusion.1 = bf16[304,5120]{1,0:T(8,128)(2,1)S(1)} fusion(bf16[152,5120]{1,0:T(8,128)(2,1)} %collective-permute-done.6, bf16[152,5120]{1,0:T(8,128)(2,1)S(1)} %copy-done.1), kind=kLoop, calls=%fused_computation.4 | loop fusion | flops 6225920 | bytes 6225920 | tf_op jit(solution)/shard_map/concatenate | solution.py:141
  83.3 6.7 %collective-permute-done.3.refs_0_ = bf16[4,320,256]{2,1,0:T(8,128)(2,1)S(1)} collective-permute-done((bf16[4,320,256]{2,1,0:T(8,128)(2,1)S(1)}, bf16[4,320,256]{2,1,0:T(8,128)(2,1)S(1)}, u32[]{:S(2)}, u32[]{:S(2)}) %collective-permute-start.3) | collective-permute-done | bytes 655392 | tf_op jit(solution)/shard_map/ppermute | solution.py:131
  92.9 3.5 %all-to-all-start.1 = ((f32[16,1,768]{2,1,0:T(1,128)}), f32[16,1,768]{2,1,0:T(1,128)S(1)}, u32[]{:S(2)}, u32[]{:S(2)}) async-start(f32[16,1,768]{2,1,0:T(1,128)} %broadcast_in_dim.111), calls=%async_computation.1 | async-start | bytes 98304 | tf_op jit(solution)/shard_map/all_to_all | solution.py:40
  96.5 5.3 %collective-permute-start.8 = (bf16[5120,256]{1,0:T(8,128)(2,1)S(1)}, bf16[5120,256]{1,0:T(8,128)(2,1)}, u32[]{:S(2)}, u32[]{:S(2)}) collective-permute-start(bf16[5120,256]{1,0:T(8,128)(2,1)S(1)} %bitcast.48), channel_id=1, source_target_pairs={{0,16},{16,0},{1,17},{17,1},{2,18},{18,2},{3,19},{19,3},{4,20},{20... | collective-permute-start | bytes 7864328 | tf_op jit(solution)/shard_map/ppermute | solution.py:147
  101.8 1.1 all-to-all-done.1
  103.7 6.4 %all-to-all-start.2 = ((f32[16,1,768]{2,1,0:T(1,128)}), f32[16,1,768]{2,1,0:T(1,128)S(1)}, u32[]{:S(2)}, u32[]{:S(2)}) async-start(f32[16,1,768]{2,1,0:T(1,128)} %broadcast_in_dim.113), calls=%async_computation.2 | async-start | bytes 98304 | tf_op jit(solution)/shard_map/all_to_all | solution.py:40
  110.6 11.1 %all-to-all-done.2 = f32[16,1,768]{2,1,0:T(1,128)S(1)} async-done(((f32[16,1,768]{2,1,0:T(1,128)}), f32[16,1,768]{2,1,0:T(1,128)S(1)}, u32[]{:S(2)}, u32[]{:S(2)}) %all-to-all-start.2) | async-done | bytes 49184 | tf_op jit(solution)/shard_map/all_to_all | solution.py:40
  122.7 7.5 %all-gather.1 = bf16[304,256]{1,0:T(8,128)(2,1)S(1)} all-gather(bf16[152,256]{1,0:T(8,128)(2,1)S(1)} %slice.117), channel_id=3, replica_groups=mesh['z'=16,'core'=2,'x'=4,'y'=4] {'core'}, dimensions={0}, use_global_device_ids=true | all-gather | bytes 233472 | tf_op jit(solution)/shard_map/all_gather | solution.py:168
  130.2 1.0 fusion.6
  131.2 1.9 %negate_select_fusion = bf16[5120,256]{1,0:T(8,128)(2,1)S(1)} fusion(bf16[5120,256]{1,0:T(8,128)(2,1)} %collective-permute-done.8, pred[]{:T(512)S(6)} %ge.3), kind=kLoop, calls=%fused_computation.2 | loop fusion | flops 2621440 | bytes 5242881 | tf_op jit(solution)/shard_map/jit(_where)/select_n | solution.py:171
  133.1 2.2 %fusion = bf16[152,5120]{1,0:T(8,128)(2,1)} fusion(f32[152,5120]{1,0:T(8,128)S(1)} %fusion.6, bf16[5120,256]{1,0:T(8,128)(2,1)S(1)} %negate_select_fusion, bf16[2,152,256]{2,1,0:T(8,128)(2,1)S(1)} %bitcast.52, s32[]{:T(128)S(6)} %select_n.148), kind=kOutput, calls=%fused_computation.1 | convolution fusion | flops 400015360 | bytes 7368708 | tf_op jit(solution)/shard_map/dot_general | solution.py:172
  (75 shorter events, 9.3 us)
Async XLA Ops:
  43.4 5.4 %copy-start = (bf16[152,5120]{1,0:T(8,128)(2,1)S(1)}, bf16[152,5120]{1,0:T(8,128)(2,1)}, u32[]{:S(2)}) copy-start(bf16[152,5120]{1,0:T(8,128)(2,1)} %param.7) | copy-start | bytes 4669444
  43.5 9.7 %copy-start.2 = (s32[32,3]{0,1:T(4,128)S(1)}, s32[32,3]{0,1:T(4,128)}, u32[]{:S(2)}) copy-start(s32[32,3]{0,1:T(4,128)} %param.9) | copy-start | bytes 1156
  44.7 15.6 %all-to-all-start = ((bf16[4,2,320,256]{3,2,1,0:T(8,128)(2,1)}), bf16[4,2,320,256]{3,2,1,0:T(8,128)(2,1)S(1)}, u32[]{:S(2)}, u32[]{:S(2)}) async-start(bf16[4,2,320,256]{3,2,1,0:T(8,128)(2,1)} %broadcast_in_dim.110), calls=%async_computation | async-start | bytes 2621440 | tf_op jit(solution)/shard_map/all_to_all | solution.py:64
  48.9 21.2 %collective-permute-start.1 = (bf16[152,5120]{1,0:T(8,128)(2,1)S(1)}, bf16[152,5120]{1,0:T(8,128)(2,1)}, u32[]{:S(2)}, u32[]{:S(2)}) collective-permute-start(bf16[152,5120]{1,0:T(8,128)(2,1)S(1)} %copy-done), channel_id=1, source_target_pairs={{0,16},{16,0},{1,17},{17,1},{2,18},{18,2},{3,19},{19,3},{4,20},{20... | collective-permute-start | bytes 4669448 | tf_op jit(solution)/shard_map/ppermute | solution.py:122
  51.0 25.7 %collective-permute-start.6 = (bf16[152,5120]{1,0:T(8,128)(2,1)}, bf16[152,5120]{1,0:T(8,128)(2,1)}, u32[]{:S(2)}, u32[]{:S(2)}) collective-permute-start(bf16[152,5120]{1,0:T(8,128)(2,1)} %param.8), channel_id=1, source_target_pairs={{0,16},{16,0},{1,17},{17,1},{2,18},{18,2},{3,19},{19,3},{4,20},{20... | collective-permute-start | bytes 4669448 | tf_op jit(solution)/shard_map/ppermute | solution.py:123
  60.4 12.8 %collective-permute-start = (bf16[4,320,256]{2,1,0:T(8,128)(2,1)S(1)}, bf16[4,320,256]{2,1,0:T(8,128)(2,1)S(1)}, u32[]{:S(2)}, u32[]{:S(2)}) collective-permute-start(bf16[4,320,256]{2,1,0:T(8,128)(2,1)S(1)} %get-tuple-element.26.refs_0_), channel_id=1, source_target_pairs={{0,1},{1,2},{2,3},{3,0},{4,5},{5,6},{6,7},{7,4},{8,9},{9,10},{10,1... | collective-permute-start | bytes 1966088 | tf_op jit(solution)/shard_map/ppermute | solution.py:131
  63.3 13.5 %collective-permute-start.5 = (bf16[4,320,256]{2,1,0:T(8,128)(2,1)S(1)}, bf16[4,320,256]{2,1,0:T(8,128)(2,1)S(1)}, u32[]{:S(2)}, u32[]{:S(2)}) collective-permute-start(bf16[4,320,256]{2,1,0:T(8,128)(2,1)S(1)} %get-tuple-element.25.refs_0_), channel_id=1, source_target_pairs={{0,3},{1,0},{2,1},{3,2},{4,7},{5,4},{6,5},{7,6},{8,11},{9,8},{10,9... | collective-permute-start | bytes 1966088 | tf_op jit(solution)/shard_map/ppermute | solution.py:131
  67.1 14.3 %copy-start.1 = (bf16[152,5120]{1,0:T(8,128)(2,1)S(1)}, bf16[152,5120]{1,0:T(8,128)(2,1)}, u32[]{:S(2)}) copy-start(bf16[152,5120]{1,0:T(8,128)(2,1)} %param.8) | copy-start | bytes 4669444
  67.1 15.9 %collective-permute-start.2 = (bf16[4,320,256]{2,1,0:T(8,128)(2,1)S(1)}, bf16[4,320,256]{2,1,0:T(8,128)(2,1)S(1)}, u32[]{:S(2)}, u32[]{:S(2)}) collective-permute-start(bf16[4,320,256]{2,1,0:T(8,128)(2,1)S(1)} %get-tuple-element.26.refs_0_), channel_id=1, source_target_pairs={{0,3},{1,0},{2,1},{3,2},{4,7},{5,4},{6,5},{7,6},{8,11},{9,8},{10,9... | collective-permute-start | bytes 1966088 | tf_op jit(solution)/shard_map/ppermute | solution.py:131
  70.1 13.0 %collective-permute-start.4 = (bf16[4,320,256]{2,1,0:T(8,128)(2,1)S(1)}, bf16[4,320,256]{2,1,0:T(8,128)(2,1)S(1)}, u32[]{:S(2)}, u32[]{:S(2)}) collective-permute-start(bf16[4,320,256]{2,1,0:T(8,128)(2,1)S(1)} %get-tuple-element.25.refs_0_), channel_id=1, source_target_pairs={{0,1},{1,2},{2,3},{3,0},{4,5},{5,6},{6,7},{7,4},{8,9},{9,10},{10,1... | collective-permute-start | bytes 1966088 | tf_op jit(solution)/shard_map/ppermute | solution.py:131
  73.2 16.7 %collective-permute-start.3 = (bf16[4,320,256]{2,1,0:T(8,128)(2,1)S(1)}, bf16[4,320,256]{2,1,0:T(8,128)(2,1)S(1)}, u32[]{:S(2)}, u32[]{:S(2)}) collective-permute-start(bf16[4,320,256]{2,1,0:T(8,128)(2,1)S(1)} %collective-permute-done.refs_1_), channel_id=1, source_target_pairs={{0,1},{1,2},{2,3},{3,0},{4,5},{5,6},{6,7},{7,4},{8,9},{9,10},{10,1... | collective-permute-start | bytes 1966088 | tf_op jit(solution)/shard_map/ppermute | solution.py:131
  76.8 14.3 %collective-permute-start.7 = (bf16[4,320,256]{2,1,0:T(8,128)(2,1)S(1)}, bf16[4,320,256]{2,1,0:T(8,128)(2,1)S(1)}, u32[]{:S(2)}, u32[]{:S(2)}) collective-permute-start(bf16[4,320,256]{2,1,0:T(8,128)(2,1)S(1)} %collective-permute-done.5.refs_2_), channel_id=1, source_target_pairs={{0,3},{1,0},{2,1},{3,2},{4,7},{5,4},{6,5},{7,6},{8,11},{9,8},{10,9... | collective-permute-start | bytes 1966088 | tf_op jit(solution)/shard_map/ppermute | solution.py:131
  92.9 9.9 %all-to-all-start.1 = ((f32[16,1,768]{2,1,0:T(1,128)}), f32[16,1,768]{2,1,0:T(1,128)S(1)}, u32[]{:S(2)}, u32[]{:S(2)}) async-start(f32[16,1,768]{2,1,0:T(1,128)} %broadcast_in_dim.111), calls=%async_computation.1 | async-start | bytes 98304 | tf_op jit(solution)/shard_map/all_to_all | solution.py:40
  96.5 34.7 %collective-permute-start.8 = (bf16[5120,256]{1,0:T(8,128)(2,1)S(1)}, bf16[5120,256]{1,0:T(8,128)(2,1)}, u32[]{:S(2)}, u32[]{:S(2)}) collective-permute-start(bf16[5120,256]{1,0:T(8,128)(2,1)S(1)} %bitcast.48), channel_id=1, source_target_pairs={{0,16},{16,0},{1,17},{17,1},{2,18},{18,2},{3,19},{19,3},{4,20},{20... | collective-permute-start | bytes 7864328 | tf_op jit(solution)/shard_map/ppermute | solution.py:147
  103.7 18.0 %all-to-all-start.2 = ((f32[16,1,768]{2,1,0:T(1,128)}), f32[16,1,768]{2,1,0:T(1,128)S(1)}, u32[]{:S(2)}, u32[]{:S(2)}) async-start(f32[16,1,768]{2,1,0:T(1,128)} %broadcast_in_dim.113), calls=%async_computation.2 | async-start | bytes 98304 | tf_op jit(solution)/shard_map/all_to_all | solution.py:40
